TPU v7x, 32 devices: a whole 2x2x4 slice. The times are simulated.
32 devices in a mesh: sample: 2 (over y), space: 16 (over z, x, core).
Axes of the slice: x: 2, y: 2, z: 4, core: 2. Of those that a mesh axis runs over, the one named last changes fastest.
Arguments:
- volume: bfloat16 [32, 2, 32, 1024], P('space', 'sample'), may hold values from -6 to 6
- out_grads: bfloat16 [16, 2, 128, 256], P('space', 'sample'), may hold values from -6 to 6
- kernel_one: bfloat16 [27, 32, 64], replicated, may hold values from -0.21875 to 0.21875
- kernel_two: bfloat16 [27, 64, 128], replicated, may hold values from -0.15625 to 0.15625
Outputs:
- layer_out: bfloat16 [16, 2, 128, 256], P('space', 'sample')
- input_grads: bfloat16 [32, 2, 32, 1024], P('space', 'sample')
- kernel_one_grads: float32 [27, 32, 64], replicated
- kernel_two_grads: float32 [27, 64, 128], replicated
All inputs are finite; a program needn't handle non-finite values.
Results may differ from a plain program's by a relative error of at most 0.015.
Values may be sent and summed in bfloat16 or wider, within the bound.
A program may use at most 128 MiB of HBM per device.

v0:
```python
import jax
import jax.numpy as jnp
from jax import lax
from jax.sharding import PartitionSpec as P

SIDE = 32


def with_halo(block, sides, width):
    for axis, dim in sides:
        count = lax.axis_size(axis)
        forward = [(i, i + 1) for i in range(count - 1)]
        backward = [(target, source) for source, target in forward]
        low = lax.ppermute(
            lax.slice_in_dim(block, block.shape[dim] - width, None, axis=dim), axis, forward
        )
        high = lax.ppermute(lax.slice_in_dim(block, 0, width, axis=dim), axis, backward)
        block = jnp.concatenate([low, block, high], axis=dim)
    return block


def passed_along(block, axis, distance):
    devices = range(lax.axis_size(axis))
    route = [(i - distance, i) for i in devices if i - distance in devices]
    return lax.ppermute(block, axis, route)


def convolve(inputs, kernel, stride, margins, dilation):
    return lax.conv_general_dilated(
        inputs,
        kernel,
        (stride, stride, stride),
        margins,
        lhs_dilation=(dilation, dilation, dilation),
        dimension_numbers=("DNCHW", "DHWIO", "DNCHW"),
        preferred_element_type=jnp.float32,
    )


def kernel_cube(kernel):
    return kernel.reshape(3, 3, 3, kernel.shape[1], kernel.shape[2])


def reversed_kernel(kernel):
    cube = kernel_cube(kernel)
    return jnp.transpose(cube[::-1, ::-1, ::-1], (0, 1, 2, 4, 3))


def weight_grad(padded, grads, stride):
    depth_out, rows_out, cols_out = (grads.shape[0], grads.shape[3], grads.shape[4])
    terms = []
    for depth_tap in range(3):
        for row_tap in range(3):
            for col_tap in range(3):
                window = lax.slice(
                    padded,
                    (depth_tap, 0, 0, row_tap, col_tap),
                    (
                        depth_tap + stride * (depth_out - 1) + 1,
                        padded.shape[1],
                        padded.shape[2],
                        row_tap + stride * (rows_out - 1) + 1,
                        col_tap + stride * (cols_out - 1) + 1,
                    ),
                    (stride, 1, 1, stride, stride),
                )
                terms.append(
                    jnp.einsum("zbiyx,zboyx->io", window, grads, preferred_element_type=jnp.float32)
                )
    return jnp.stack(terms)


def local(volume, out_grads, kernel_one, kernel_two):
    depth, batch, channels_in, plane = volume.shape
    channels_two = kernel_two.shape[2]
    half_side = SIDE // 2
    space_count = lax.axis_size("space")
    sample_count = lax.axis_size("sample")
    scale_one = float(sample_count * batch * space_count * depth * plane) ** (-0.5)
    scale_two = scale_one * 8.0**0.5
    cells = volume.reshape(depth, batch, channels_in, SIDE, SIDE)
    grads_cells = out_grads.reshape(depth // 2, batch, channels_two, half_side, half_side)
    framed = with_halo(cells, (("space", 0),), 1)
    pre_one = convolve(framed, kernel_cube(kernel_one), 1, [(0, 0), (1, 1), (1, 1)], 1)
    hidden = jax.nn.silu(pre_one).astype(jnp.bfloat16)
    below = passed_along(hidden[-1:], "space", 1)
    stacked = jnp.pad(jnp.concatenate([below, hidden], 0), ((0, 0), (0, 0), (0, 0), (1, 1), (1, 1)))
    strided = convolve(stacked, kernel_cube(kernel_two), 2, [(0, 0), (0, 0), (0, 0)], 1)
    above = passed_along(grads_cells, "space", -1)
    spread = convolve(
        jnp.concatenate([grads_cells, above], 0),
        reversed_kernel(kernel_two),
        1,
        [(1, 0), (1, 2), (1, 2)],
        2,
    )
    hidden_grads = spread.astype(jnp.bfloat16)
    local_two = weight_grad(stacked, grads_cells, 2) * scale_two
    second_grads = lax.psum(local_two, ("sample", "space"))
    layer_out = strided.astype(jnp.bfloat16).reshape(depth // 2, batch, channels_two, plane // 4)
    sigma = jax.nn.sigmoid(pre_one)
    pre_grads = (hidden_grads.astype(jnp.float32) * sigma * (1.0 + pre_one * (1.0 - sigma))).astype(
        jnp.bfloat16
    )
    framed_grads = with_halo(pre_grads, (("space", 0),), 1)
    input_grads = convolve(
        framed_grads, reversed_kernel(kernel_one), 1, [(0, 0), (1, 1), (1, 1)], 1
    ).astype(jnp.bfloat16)
    padded_input = jnp.pad(framed, ((0, 0), (0, 0), (0, 0), (1, 1), (1, 1)))
    first_grads = weight_grad(padded_input, pre_grads, 1) * scale_one
    first_grads = lax.psum(first_grads, ("sample", "space"))
    return (
        layer_out,
        input_grads.reshape(depth, batch, channels_in, plane),
        first_grads,
        second_grads,
    )


def solution(mesh):
    in_specs = (P("space", "sample", None, None), P("space", "sample", None, None), P(), P())
    out_specs = (P("space", "sample", None, None), P("space", "sample", None, None), P(), P())
    return jax.shard_map(local, mesh=mesh, in_specs=in_specs, out_specs=out_specs, check_vma=False)
```

profile of v0, /device:TPU:0, one launch (start us, length us, event | category | flops | bytes accessed | tf_op | source)
XLA Modules:
  0.0 335.2 jit_solution(12006026243020860200)
XLA Ops:
  7.2 0.9 fusion.282
  8.8 1.3 collective-permute-start.1
  10.8 3.0 collective-permute-start
  13.9 1.3 collective-permute-start.3
  16.0 0.9 copy.120
  16.9 1.6 copy.157
  19.6 1.6 copy.123
  21.2 1.2 slice.285
  22.5 3.8 %add_divide_fusion = (f32[2,32,8,5,64]{4,2,3,1,0:T(8,128)S(1)}, f32[2,32,8,5,64]{4,2,3,1,0:T(8,128)S(1)}, bf16[2,32,8,5,64]{4,2,3,1,0:T(8,128)(2,1)S(1)}) fusion(bf16[3,3,3,32,64]{4,3,2,1,0:T(8,128)(2,1)S(1)} %bitcast.718, bf16[4,32,32,1,7,2]{1,4,5,2,0,3:T(8,128)(2,1)S(1)} %slice.285, bf16[4,32,32,1,8,5]{1,4,5,2,0,3:T(8,128)(2,1)} %copy.123, ...), kind=kOutput, calls=%fused_computation.31 | convolution fusion | flops 280068096 | bytes 2191400 | tf_op jit(solution)/shard_map/conv_general_dilated | solution.py:29
  26.5 5.1 %collective-permute-start.2 = (bf16[1,1,64,32,32]{2,3,4,1,0:T(8,128)(2,1)S(1)}, bf16[1,1,64,32,32]{2,3,4,1,0:T(8,128)(2,1)S(1)}, u32[]{:S(2)}, u32[]{:S(2)}) collective-permute-start(bf16[1,1,64,32,32]{2,3,4,1,0:T(8,128)(2,1)S(1)} %slice_bitcast_fusion.2), channel_id=1, source_target_pairs={{0,1},{1,2},{2,3},{3,4},{4,5},{5,6},{6,7},{7,8},{8,9},{9,10},{10,1... | collective-permute-start | bytes 393224 | tf_op jit(solution)/shard_map/ppermute | solution.py:25
  32.8 0.8 fusion.24
  34.6 1.3 collective-permute-start.5
  35.9 5.0 %collective-permute-start.4 = (bf16[1,1,64,32,32]{2,3,4,0,1:T(8,128)(2,1)S(1)}, bf16[1,1,64,32,32]{2,3,4,0,1:T(8,128)(2,1)}, u32[]{:S(2)}, u32[]{:S(2)}) collective-permute-start(bf16[1,1,64,32,32]{2,3,4,0,1:T(8,128)(2,1)S(1)} %get-tuple-element.21), channel_id=1, source_target_pairs={{0,1},{1,2},{2,3},{3,4},{4,5},{5,6},{6,7},{7,8},{8,9},{9,10},{10,1... | collective-permute-start | bytes 393224 | tf_op jit(solution)/shard_map/ppermute | solution.py:14
  41.4 0.6 fusion.92
  42.0 0.6 fusion.91
  43.9 0.6 fusion.87
  45.1 0.6 fusion.85
  45.6 0.6 fusion.84
  46.8 0.6 fusion.82
  48.6 0.6 fusion.79
  49.1 0.6 fusion.78
  49.7 0.6 fusion.77
  50.3 0.6 fusion.76
  50.8 0.6 fusion.75
  51.4 0.6 fusion.74
  53.2 0.6 fusion.70
  54.3 0.6 fusion.68
  54.9 0.8 broadcast_multiply_fusion.1
  56.2 5.1 %slice.246 = bf16[1,1,64,16,16]{2,3,4,1,0:T(8,128)(2,1)} slice(bf16[3,1,64,34,34]{2,3,4,1,0:T(8,128)(2,1)S(1)} %pad.9), slice={[0:1:1], [0:1:1], [0:64:1], [0:31:2], [0:31:2]} | slice | bytes 65536 | tf_op jit(solution)/shard_map/slice | solution.py:55
  61.4 4.9 %slice.247 = bf16[1,1,64,16,16]{2,3,4,1,0:T(8,128)(2,1)} slice(bf16[3,1,64,34,34]{2,3,4,1,0:T(8,128)(2,1)S(1)} %pad.9), slice={[0:1:1], [0:1:1], [0:64:1], [0:31:2], [1:32:2]} | slice | bytes 65536 | tf_op jit(solution)/shard_map/slice | solution.py:55
  66.2 4.9 %slice.248 = bf16[1,1,64,16,16]{2,3,4,1,0:T(8,128)(2,1)} slice(bf16[3,1,64,34,34]{2,3,4,1,0:T(8,128)(2,1)S(1)} %pad.9), slice={[0:1:1], [0:1:1], [0:64:1], [0:31:2], [2:33:2]} | slice | bytes 65536 | tf_op jit(solution)/shard_map/slice | solution.py:55
  71.1 4.9 %slice.249 = bf16[1,1,64,16,16]{2,3,4,1,0:T(8,128)(2,1)} slice(bf16[3,1,64,34,34]{2,3,4,1,0:T(8,128)(2,1)S(1)} %pad.9), slice={[0:1:1], [0:1:1], [0:64:1], [1:32:2], [0:31:2]} | slice | bytes 65536 | tf_op jit(solution)/shard_map/slice | solution.py:55
  76.0 4.9 %slice.250 = bf16[1,1,64,16,16]{2,3,4,1,0:T(8,128)(2,1)} slice(bf16[3,1,64,34,34]{2,3,4,1,0:T(8,128)(2,1)S(1)} %pad.9), slice={[0:1:1], [0:1:1], [0:64:1], [1:32:2], [1:32:2]} | slice | bytes 65536 | tf_op jit(solution)/shard_map/slice | solution.py:55
  80.9 4.9 %slice.251 = bf16[1,1,64,16,16]{2,3,4,1,0:T(8,128)(2,1)} slice(bf16[3,1,64,34,34]{2,3,4,1,0:T(8,128)(2,1)S(1)} %pad.9), slice={[0:1:1], [0:1:1], [0:64:1], [1:32:2], [2:33:2]} | slice | bytes 65536 | tf_op jit(solution)/shard_map/slice | solution.py:55
  85.8 4.9 %slice.252 = bf16[1,1,64,16,16]{2,3,4,1,0:T(8,128)(2,1)} slice(bf16[3,1,64,34,34]{2,3,4,1,0:T(8,128)(2,1)S(1)} %pad.9), slice={[0:1:1], [0:1:1], [0:64:1], [2:33:2], [0:31:2]} | slice | bytes 65536 | tf_op jit(solution)/shard_map/slice | solution.py:55
  90.6 4.9 %slice.253 = bf16[1,1,64,16,16]{2,3,4,1,0:T(8,128)(2,1)} slice(bf16[3,1,64,34,34]{2,3,4,1,0:T(8,128)(2,1)S(1)} %pad.9), slice={[0:1:1], [0:1:1], [0:64:1], [2:33:2], [1:32:2]} | slice | bytes 65536 | tf_op jit(solution)/shard_map/slice | solution.py:55
  95.5 4.9 %slice.254 = bf16[1,1,64,16,16]{2,3,4,1,0:T(8,128)(2,1)} slice(bf16[3,1,64,34,34]{2,3,4,1,0:T(8,128)(2,1)S(1)} %pad.9), slice={[0:1:1], [0:1:1], [0:64:1], [2:33:2], [2:33:2]} | slice | bytes 65536 | tf_op jit(solution)/shard_map/slice | solution.py:55
  100.4 4.9 %slice.255 = bf16[1,1,64,16,16]{2,3,4,1,0:T(8,128)(2,1)} slice(bf16[3,1,64,34,34]{2,3,4,1,0:T(8,128)(2,1)S(1)} %pad.9), slice={[1:2:1], [0:1:1], [0:64:1], [0:31:2], [0:31:2]} | slice | bytes 65536 | tf_op jit(solution)/shard_map/slice | solution.py:55
  105.3 4.9 %slice.256 = bf16[1,1,64,16,16]{2,3,4,1,0:T(8,128)(2,1)} slice(bf16[3,1,64,34,34]{2,3,4,1,0:T(8,128)(2,1)S(1)} %pad.9), slice={[1:2:1], [0:1:1], [0:64:1], [0:31:2], [1:32:2]} | slice | bytes 65536 | tf_op jit(solution)/shard_map/slice | solution.py:55
  110.2 4.9 %slice.257 = bf16[1,1,64,16,16]{2,3,4,1,0:T(8,128)(2,1)} slice(bf16[3,1,64,34,34]{2,3,4,1,0:T(8,128)(2,1)S(1)} %pad.9), slice={[1:2:1], [0:1:1], [0:64:1], [0:31:2], [2:33:2]} | slice | bytes 65536 | tf_op jit(solution)/shard_map/slice | solution.py:55
  115.1 4.9 %slice.258 = bf16[1,1,64,16,16]{2,3,4,1,0:T(8,128)(2,1)} slice(bf16[3,1,64,34,34]{2,3,4,1,0:T(8,128)(2,1)S(1)} %pad.9), slice={[1:2:1], [0:1:1], [0:64:1], [1:32:2], [0:31:2]} | slice | bytes 65536 | tf_op jit(solution)/shard_map/slice | solution.py:55
  119.9 4.9 %slice.259 = bf16[1,1,64,16,16]{2,3,4,1,0:T(8,128)(2,1)} slice(bf16[3,1,64,34,34]{2,3,4,1,0:T(8,128)(2,1)S(1)} %pad.9), slice={[1:2:1], [0:1:1], [0:64:1], [1:32:2], [1:32:2]} | slice | bytes 65536 | tf_op jit(solution)/shard_map/slice | solution.py:55
  124.8 4.9 %slice.260 = bf16[1,1,64,16,16]{2,3,4,1,0:T(8,128)(2,1)} slice(bf16[3,1,64,34,34]{2,3,4,1,0:T(8,128)(2,1)S(1)} %pad.9), slice={[1:2:1], [0:1:1], [0:64:1], [1:32:2], [2:33:2]} | slice | bytes 65536 | tf_op jit(solution)/shard_map/slice | solution.py:55
  129.7 4.9 %slice.261 = bf16[1,1,64,16,16]{2,3,4,1,0:T(8,128)(2,1)} slice(bf16[3,1,64,34,34]{2,3,4,1,0:T(8,128)(2,1)S(1)} %pad.9), slice={[1:2:1], [0:1:1], [0:64:1], [2:33:2], [0:31:2]} | slice | bytes 65536 | tf_op jit(solution)/shard_map/slice | solution.py:55
  134.6 4.9 %slice.262 = bf16[1,1,64,16,16]{2,3,4,1,0:T(8,128)(2,1)} slice(bf16[3,1,64,34,34]{2,3,4,1,0:T(8,128)(2,1)S(1)} %pad.9), slice={[1:2:1], [0:1:1], [0:64:1], [2:33:2], [1:32:2]} | slice | bytes 65536 | tf_op jit(solution)/shard_map/slice | solution.py:55
  139.4 4.9 %slice.263 = bf16[1,1,64,16,16]{2,3,4,1,0:T(8,128)(2,1)} slice(bf16[3,1,64,34,34]{2,3,4,1,0:T(8,128)(2,1)S(1)} %pad.9), slice={[1:2:1], [0:1:1], [0:64:1], [2:33:2], [2:33:2]} | slice | bytes 65536 | tf_op jit(solution)/shard_map/slice | solution.py:55
  144.3 4.9 %slice.264 = bf16[1,1,64,16,16]{2,3,4,1,0:T(8,128)(2,1)} slice(bf16[3,1,64,34,34]{2,3,4,1,0:T(8,128)(2,1)S(1)} %pad.9), slice={[2:3:1], [0:1:1], [0:64:1], [0:31:2], [0:31:2]} | slice | bytes 65536 | tf_op jit(solution)/shard_map/slice | solution.py:55
  149.2 4.9 %slice.265 = bf16[1,1,64,16,16]{2,3,4,1,0:T(8,128)(2,1)} slice(bf16[3,1,64,34,34]{2,3,4,1,0:T(8,128)(2,1)S(1)} %pad.9), slice={[2:3:1], [0:1:1], [0:64:1], [0:31:2], [1:32:2]} | slice | bytes 65536 | tf_op jit(solution)/shard_map/slice | solution.py:55
  154.0 4.9 %slice.266 = bf16[1,1,64,16,16]{2,3,4,1,0:T(8,128)(2,1)} slice(bf16[3,1,64,34,34]{2,3,4,1,0:T(8,128)(2,1)S(1)} %pad.9), slice={[2:3:1], [0:1:1], [0:64:1], [0:31:2], [2:33:2]} | slice | bytes 65536 | tf_op jit(solution)/shard_map/slice | solution.py:55
  158.9 4.9 %slice.267 = bf16[1,1,64,16,16]{2,3,4,1,0:T(8,128)(2,1)} slice(bf16[3,1,64,34,34]{2,3,4,1,0:T(8,128)(2,1)S(1)} %pad.9), slice={[2:3:1], [0:1:1], [0:64:1], [1:32:2], [0:31:2]} | slice | bytes 65536 | tf_op jit(solution)/shard_map/slice | solution.py:55
  163.8 4.9 %slice.268 = bf16[1,1,64,16,16]{2,3,4,1,0:T(8,128)(2,1)} slice(bf16[3,1,64,34,34]{2,3,4,1,0:T(8,128)(2,1)S(1)} %pad.9), slice={[2:3:1], [0:1:1], [0:64:1], [1:32:2], [1:32:2]} | slice | bytes 65536 | tf_op jit(solution)/shard_map/slice | solution.py:55
  168.7 4.9 %slice.269 = bf16[1,1,64,16,16]{2,3,4,1,0:T(8,128)(2,1)} slice(bf16[3,1,64,34,34]{2,3,4,1,0:T(8,128)(2,1)S(1)} %pad.9), slice={[2:3:1], [0:1:1], [0:64:1], [1:32:2], [2:33:2]} | slice | bytes 65536 | tf_op jit(solution)/shard_map/slice | solution.py:55
  173.6 4.9 %slice.270 = bf16[1,1,64,16,16]{2,3,4,1,0:T(8,128)(2,1)} slice(bf16[3,1,64,34,34]{2,3,4,1,0:T(8,128)(2,1)S(1)} %pad.9), slice={[2:3:1], [0:1:1], [0:64:1], [2:33:2], [0:31:2]} | slice | bytes 65536 | tf_op jit(solution)/shard_map/slice | solution.py:55
  179.5 0.8 copy.128
  180.4 0.6 fusion.37
  181.1 0.7 copy.200
  181.9 1.3 maximum_bitcast_fusion
  189.6 1.0 broadcast_multiply_fusion
  190.6 4.7 %fusion.31 = bf16[2,32,8,5,32]{4,2,3,1,0:T(8,128)(2,1)S(1)} fusion(bf16[3,3,3,32,64]{4,3,2,1,0:T(8,128)(2,1)S(1)} %bitcast.719, bf16[4,64,32,1,7,2]{1,4,5,2,0,3:T(8,128)(2,1)S(1)} %slice.297, bf16[4,64,32,1,8,5]{1,4,5,2,0,3:T(8,128)(2,1)S(1)} %copy.139, pred[8,5]{0,1:T(8,128)(4,1)S(1)} %copy-done.38), kind=kOutput, calls=%fused_computation.28 | convolution fusion | flops 280133632 | bytes 1159208 | tf_op jit(solution)/shard_map/conv_general_dilated | solution.py:29
  195.5 1.1 copy.141
  196.6 1.2 reshape.283
  197.8 127.8 %all-reduce.5.cloned.1.call-done = (f32[27,32,64]{2,1,0:T(8,128)}, f32[27,64,128]{2,1,0:T(8,128)}) async-done(((f32[27,32,64]{2,1,0:T(8,128)}, f32[27,64,128]{2,1,0:T(8,128)}), (f32[27,32,64]{2,1,0:T(8,128)}, f32[27,64,128]{2,1,0:T(8,128)})) %all-reduce.5.cloned.1.call-update) | async-done | bytes 1105936 | tf_op jit(solution)/shard_map/psum | solution.py:111
  325.5 1.9 copy.393
  327.4 0.9 copy.394
  (169 shorter events, 19.3 us)
Async XLA Ops:
  7.2 25.2 %copy-start = (bf16[27,64,128]{2,1,0:T(8,128)(2,1)S(1)}, bf16[27,64,128]{2,1,0:T(8,128)(2,1)}, u32[]{:S(2)}) copy-start(bf16[27,64,128]{2,1,0:T(8,128)(2,1)} %param.7) | copy-start | bytes 1327108
  7.2 8.1 %copy-start.4 = (bf16[2,1,32,1024]{3,2,1,0:T(8,128)(2,1)S(1)}, bf16[2,1,32,1024]{3,2,1,0:T(8,128)(2,1)}, u32[]{:S(2)}) copy-start(bf16[2,1,32,1024]{3,2,1,0:T(8,128)(2,1)} %param.4) | copy-start | bytes 393220
  7.2 6.6 %copy-start.10 = (bf16[1,1,128,256]{3,2,1,0:T(8,128)(2,1)S(1)}, bf16[1,1,128,256]{3,2,1,0:T(8,128)(2,1)}, u32[]{:S(2)}) copy-start(bf16[1,1,128,256]{3,2,1,0:T(8,128)(2,1)} %param.5) | copy-start | bytes 196612
  7.2 318.3 %all-reduce.5.cloned.1.call-start = ((), (), s32[]{:S(2)}) async-start(), calls=%async_computation | async-start | bytes 2654208 | tf_op jit(solution)/shard_map/psum | solution.py:111
  8.8 9.6 %collective-permute-start.1 = (bf16[1,1,32,32,32]{3,2,0,4,1:T(8,128)(2,1)S(1)}, bf16[1,1,32,32,32]{3,2,0,4,1:T(8,128)(2,1)S(1)}, u32[]{:S(2)}, u32[]{:S(2)}) collective-permute-start(bf16[1,1,32,32,32]{3,2,0,4,1:T(8,128)(2,1)S(1)} %copy.119), channel_id=1, source_target_pairs={{1,0},{2,1},{3,2},{4,3},{5,4},{6,5},{7,6},{8,7},{9,8},{10,9},{11,1... | collective-permute-start | bytes 196616 | tf_op jit(solution)/shard_map/ppermute | solution.py:17
  10.8 7.7 %collective-permute-start = (bf16[1,1,32,32,32]{3,2,0,4,1:T(8,128)(2,1)S(1)}, bf16[1,1,32,32,32]{3,2,0,4,1:T(8,128)(2,1)S(1)}, u32[]{:S(2)}, u32[]{:S(2)}) collective-permute-start(bf16[1,1,32,32,32]{3,2,0,4,1:T(8,128)(2,1)S(1)} %copy.118), channel_id=1, source_target_pairs={{0,1},{1,2},{2,3},{3,4},{4,5},{5,6},{6,7},{7,8},{8,9},{9,10},{10,1... | collective-permute-start | bytes 196616 | tf_op jit(solution)/shard_map/ppermute | solution.py:14
  13.9 18.2 %collective-permute-start.3 = (bf16[1,1,128,16,16]{2,4,3,1,0:T(8,128)(2,1)S(1)}, bf16[1,1,128,16,16]{2,4,3,1,0:T(8,128)(2,1)S(1)}, u32[]{:S(2)}, u32[]{:S(2)}) collective-permute-start(bf16[1,1,128,16,16]{2,4,3,1,0:T(8,128)(2,1)S(1)} %bitcast.688), channel_id=1, source_target_pairs={{1,0},{2,1},{3,2},{4,3},{5,4},{6,5},{7,6},{8,7},{9,8},{10,9},{11,1... | collective-permute-start | bytes 196616 | tf_op jit(solution)/shard_map/ppermute | solution.py:25
  16.8 1.9 copy-start.2
  18.4 0.7 copy-start.6
  18.5 0.8 copy-start.8
  19.6 2.9 copy-start.36
  19.6 2.9 copy-start.38
  26.5 29.2 %collective-permute-start.2 = (bf16[1,1,64,32,32]{2,3,4,1,0:T(8,128)(2,1)S(1)}, bf16[1,1,64,32,32]{2,3,4,1,0:T(8,128)(2,1)S(1)}, u32[]{:S(2)}, u32[]{:S(2)}) collective-permute-start(bf16[1,1,64,32,32]{2,3,4,1,0:T(8,128)(2,1)S(1)} %slice_bitcast_fusion.2), channel_id=1, source_target_pairs={{0,1},{1,2},{2,3},{3,4},{4,5},{5,6},{6,7},{7,8},{8,9},{9,10},{10,1... | collective-permute-start | bytes 393224 | tf_op jit(solution)/shard_map/ppermute | solution.py:25
  32.2 0.7 copy-start.39
  34.6 147.3 %collective-permute-start.5 = (bf16[1,1,64,32,32]{2,3,4,0,1:T(8,128)(2,1)S(1)}, bf16[1,1,64,32,32]{2,3,4,0,1:T(8,128)(2,1)}, u32[]{:S(2)}, u32[]{:S(2)}) collective-permute-start(bf16[1,1,64,32,32]{2,3,4,0,1:T(8,128)(2,1)S(1)} %get-tuple-element.22), channel_id=1, source_target_pairs={{1,0},{2,1},{3,2},{4,3},{5,4},{6,5},{7,6},{8,7},{9,8},{10,9},{11,1... | collective-permute-start | bytes 393224 | tf_op jit(solution)/shard_map/ppermute | solution.py:17
  35.9 146.0 %collective-permute-start.4 = (bf16[1,1,64,32,32]{2,3,4,0,1:T(8,128)(2,1)S(1)}, bf16[1,1,64,32,32]{2,3,4,0,1:T(8,128)(2,1)}, u32[]{:S(2)}, u32[]{:S(2)}) collective-permute-start(bf16[1,1,64,32,32]{2,3,4,0,1:T(8,128)(2,1)S(1)} %get-tuple-element.21), channel_id=1, source_target_pairs={{0,1},{1,2},{2,3},{3,4},{4,5},{5,6},{6,7},{7,8},{8,9},{9,10},{10,1... | collective-permute-start | bytes 393224 | tf_op jit(solution)/shard_map/ppermute | solution.py:14
  42.0 1.0 copy-start.3
  42.0 1.1 copy-start.9
  46.8 1.0 copy-start.1
  51.4 1.0 copy-start.7
  179.5 0.9 copy-start.40
  183.4 0.8 copy-start.35
  183.4 1.0 copy-start.34
  184.0 0.9 copy-start.33
  184.0 1.0 copy-start.32
  184.0 1.2 copy-start.31
  184.0 1.4 copy-start.30
  184.0 1.6 copy-start.29
  184.0 1.8 copy-start.28
  184.0 1.9 copy-start.27
  184.2 2.0 copy-start.26
  184.2 2.2 copy-start.25
  184.2 2.4 copy-start.24
  184.4 2.3 copy-start.23
  184.8 2.1 copy-start.22
  185.0 2.1 copy-start.21
  185.2 2.1 copy-start.20
  185.4 2.1 copy-start.19
  185.6 2.1 copy-start.18
  185.8 2.1 copy-start.17
  186.0 2.1 copy-start.16
  186.2 2.1 copy-start.15
  186.4 2.1 copy-start.14
  186.6 2.1 copy-start.13
  186.8 2.0 copy-start.12
  187.0 2.0 copy-start.11
  189.5 1.1 copy-start.37
  325.5 1.9 copy-start.5
Sparse Core Ops, SparseCore 0:
  190.7 134.7 all-reduce.4
where the time goes:
time: 336 us; the launch traced here: 335 us
  local copies, waits for them, and re-layouts  143 us (43%)
  waiting for transfers between devices  128 us (38%)
  matrix products  28.3 us (8%)
  starting transfers between devices  17 us (5%)
  between operations  15.2 us (5%)
  other arithmetic  3.87 us (1%)
    psum x1, waiting for transfers between devices, local(): first_grads = lax.psum(first_grads, ('sample', 'space'))  128 us
    slice x27, local copies, waits for them, and re-layouts, weight_grad(): lax.slice(padded, (depth_tap, 0, 0, row_tap, col_tap), (depth_tap + strid...  123 us
    dot_general x54, matrix products, weight_grad(): jnp.einsum('zbiyx,zboyx->io', window, grads, preferred_element_type=jnp.f...  18.3 us
    conv_general_dilated x4, matrix products, convolve(): lax.conv_general_dilated(inputs, kernel, (stride, stride, stride), margin...  9.99 us
    ppermute x2, starting transfers between devices, with_halo(): lax.ppermute(lax.slice_in_dim(block, block.shape[dim] - width, None, axis...  8.02 us
  transfers between devices with their start and end apart: 7, of which 1 were waited for; matrix products, arithmetic and copies ran while one was open for 48% of the time, Pallas kernels for 0%

commit v1 on v0

v1 whole, which is shorter than its diff:
```python
import functools

import jax
import jax.numpy as jnp
from jax import lax
from jax.experimental import pallas as pl
from jax.experimental.pallas import tpu as pltpu
from jax.sharding import PartitionSpec as P

F32 = jnp.float32
BF16 = jnp.bfloat16
MESH = pl.DeviceIdType.MESH
VMEM_SPEC = pl.BlockSpec(memory_space=pltpu.VMEM)
PAIR = 14
ROWS_TWO = 27 * 64
ROWS_ONE = PAIR * 32
WINDOWS = {-1: (1, -1), 0: (0, 0), 1: (1, 0), 2: (0, 1)}


def group_sizes(samples, spaces):
    return 4 * samples, spaces // 4


def padded_rows(samples, spaces):
    first, second = group_sizes(samples, spaces)
    unit = first * second * 16
    return -(-(ROWS_TWO + ROWS_ONE) // unit) * unit


def mm(a, b, dims=((1,), (0,))):
    return lax.dot_general(a, b, (dims, ((), ())), preferred_element_type=F32)


def halo_kernel(spaces, vol, og, vlo, vhi, olo, ohi, send_sem, recv_sem):
    me = lax.axis_index("space")
    sample = lax.axis_index("sample")
    barrier = pltpu.get_barrier_semaphore()
    below, above = me - 1, me + 1

    @pl.when(me > 0)
    def _():
        pl.semaphore_signal(barrier, inc=1, device_id=(sample, below), device_id_type=MESH)

    @pl.when(me < spaces - 1)
    def _():
        pl.semaphore_signal(barrier, inc=1, device_id=(sample, above), device_id_type=MESH)

    pl.semaphore_wait(barrier, jnp.minimum(me, 1) + jnp.minimum(spaces - 1 - me, 1))

    def copy(src, dst, index, target):
        return pltpu.make_async_remote_copy(
            src_ref=src,
            dst_ref=dst,
            send_sem=send_sem.at[index],
            recv_sem=recv_sem.at[index],
            device_id=(sample, target),
            device_id_type=MESH,
        )

    up = [(vol, vlo, 0), (og, olo, 1)]
    down = [(vol, vhi, 2), (og, ohi, 3)]

    @pl.when(me < spaces - 1)
    def _():
        for src, dst, index in up:
            copy(src, dst, index, above).start()

    @pl.when(me > 0)
    def _():
        for src, dst, index in down:
            copy(src, dst, index, below).start()

    @pl.when(me < spaces - 1)
    def _():
        for src, dst, index in up:
            copy(src, dst, index, above).wait_send()
        for src, dst, index in down:
            copy(src, dst, index, above).wait_recv()

    @pl.when(me > 0)
    def _():
        for src, dst, index in down:
            copy(src, dst, index, below).wait_send()
        for src, dst, index in up:
            copy(src, dst, index, below).wait_recv()


def windows(parts, lanes, us):
    cell = lax.broadcasted_iota(jnp.int32, (1, lanes), 1)
    q, r = (cell >> 4) & 15, cell & 15
    for uy in us:
        for ux in us:
            (py, sy), (px, sx) = WINDOWS[uy], WINDOWS[ux]
            part = parts(2 * py + px)
            offset = 16 * sy + sx
            if offset != 0:
                part = pltpu.roll(part, (-offset) % lanes, 1)
                inside = (q + sy >= 0) & (q + sy <= 15) & (r + sx >= 0) & (r + sx <= 15)
                part = jnp.where(inside, part, 0.0)
            yield part.astype(BF16)


def tap_block(kernel, dz, dy, dx, shape):
    if 0 <= dy <= 2 and 0 <= dx <= 2:
        return kernel[9 * dz + 3 * dy + dx]
    return jnp.zeros(shape, BF16)


def math_kernel(
    spaces, vol, vlo, vhi, og, olo, ohi, k1, k2,
    layer, igrads, grads,
    order, t1, t2, o4, tg, w1, wb, wc, hgrads,
):
    me = lax.axis_index("space")
    has_low, has_high = me > 0, me < spaces - 1

    def order_rows(step, carry):
        start = pl.multiple_of(step * 128, 128)
        col = lax.broadcasted_iota(jnp.int32, (1, 1024), 1)
        phase, q, r = col >> 8, (col >> 4) & 15, col & 15
        source = (2 * q + (phase >> 1)) * 32 + 2 * r + (phase & 1)
        row = lax.broadcasted_iota(jnp.int32, (128, 1024), 0) + start
        order[pl.ds(start, 128), :] = jnp.where(row == source, 1.0, 0.0).astype(BF16)
        return carry

    lax.fori_loop(0, 8, order_rows, 0)

    us = (-1, 0, 1, 2)
    phases = [(0, 0), (0, 1), (1, 0), (1, 1)]
    for dz in range(3):
        for index, (uy, ux) in enumerate((a, b) for a in us for b in us):
            w1[dz, 32 * index : 32 * index + 32, :] = jnp.concatenate(
                [tap_block(k1, dz, uy - py + 1, ux - px + 1, (32, 64)) for py, px in phases], axis=1
            )
        for index, (py, px) in enumerate(phases):
            wc[dz, 32 * index : 32 * index + 32, :] = jnp.concatenate(
                [tap_block(k1, dz, py + 1 - uy, px + 1 - ux, (32, 64)) for uy in us for ux in us],
                axis=1,
            )
            taps = {(0, 0): 1, (0, 1): -1, (1, 0): 2, (1, 1): 0}
            wb[dz, 64 * index : 64 * index + 64, :] = jnp.concatenate(
                [
                    tap_block(k2, dz, taps[py, sy], taps[px, sx], (64, 128))
                    for sy in (0, 1)
                    for sx in (0, 1)
                ],
                axis=1,
            )

    zero = jnp.zeros((), BF16)
    low = jnp.where(has_low, vlo[...].reshape(64, 1024), zero)
    high = jnp.where(has_high, vhi[...].reshape(64, 1024), zero)
    cells = jnp.concatenate([low, vol[...].reshape(64, 1024), high], axis=0)
    split = mm(cells, order[...])

    def volume_part(phase):
        return jnp.concatenate(
            [split[32 * p : 32 * p + 32, 256 * phase : 256 * phase + 256] for p in range(6)], axis=1
        )

    for index, part in enumerate(windows(volume_part, 1536, us)):
        t1[32 * index : 32 * index + 32, :] = part

    og_three = jnp.concatenate(
        [jnp.where(has_low, olo[...], zero), og[...], jnp.where(has_high, ohi[...], zero)], axis=1
    ).astype(F32)
    cell = lax.broadcasted_iota(jnp.int32, (1, 768), 1)
    q, r = (cell >> 4) & 15, cell & 15
    for sy in (0, 1):
        for sx in (0, 1):
            part = og_three
            if sy + sx > 0:
                part = pltpu.roll(part, 768 - 16 * sy - sx, 1)
                part = jnp.where((q + sy <= 15) & (r + sx <= 15), part, 0.0)
            index = 2 * sy + sx
            o4[128 * index : 128 * index + 128, :] = part.astype(BF16)

    even = mm(wb[1], o4[:, 256:768])
    odd = mm(wb[2], o4[:, 0:512]) + mm(wb[0], o4[:, 256:768])
    hgrads[:, 0:256] = odd[:, 0:256].astype(BF16)
    hgrads[:, 256:512] = even[:, 0:256].astype(BF16)
    hgrads[:, 512:768] = odd[:, 256:512].astype(BF16)
    hgrads[:, 768:1024] = even[:, 256:512].astype(BF16)

    tn = ((0,), (0,))
    nt = ((1,), (1,))
    pre = mm(w1[0], t1[:, 0:1024], tn)
    pre += mm(w1[1], t1[:, 256:1280], tn)
    pre += mm(w1[2], t1[:, 512:1536], tn)
    sigma = 1.0 / (1.0 + jnp.exp(-pre))
    plane = lax.broadcasted_iota(jnp.int32, (1, 1024), 1) >> 8
    real = ((plane > 0) | has_low) & ((plane < 3) | has_high)
    hidden = jnp.where(real, pre * sigma, 0.0).astype(BF16).astype(F32)
    slope = hgrads[...].astype(F32) * sigma * (1.0 + pre * (1.0 - sigma))
    pre_grads = jnp.where(real, slope, 0.0).astype(BF16)
    pre_wide = pre_grads.astype(F32)

    for index, part in enumerate(
        windows(lambda ph: hidden[64 * ph : 64 * ph + 64, 0:768], 768, (-1, 0, 1))
    ):
        t2[64 * index : 64 * index + 64, :] = part
    total = jnp.zeros((128, 256), F32)
    for dz in range(3):
        here = t2[:, 256 * dz : 256 * dz + 256]
        total += mm(k2[9 * dz : 9 * dz + 9].reshape(576, 128), here, tn)
        grads[576 * dz : 576 * dz + 576, :] = mm(here, og[...], nt).astype(BF16)
    layer[...] = total.astype(BF16)

    pairs = {}
    for dz in range(3):
        here = mm(t1[:, 256 * dz + 256 : 256 * dz + 768], pre_grads[:, 256:768], nt)
        for dy in range(3):
            for dx in range(3):
                term = None
                for index, (py, px) in enumerate(phases):
                    row = 32 * (4 * (py + dy) + px + dx)
                    block = here[row : row + 32, 64 * index : 64 * index + 64]
                    term = block if term is None else term + block
                pairs[9 * dz + 3 * dy + dx] = term
    pairs[27] = jnp.zeros((32, 64), F32)
    for tap in range(PAIR):
        grads[ROWS_TWO + 32 * tap : ROWS_TWO + 32 * tap + 32, :] = jnp.concatenate(
            [pairs[tap], pairs[tap + PAIR]], axis=1
        ).astype(BF16)
    used = ROWS_TWO + ROWS_ONE
    if grads.shape[0] > used:
        grads[used:, :] = jnp.zeros((grads.shape[0] - used, 128), BF16)

    for index, part in enumerate(
        windows(lambda ph: pre_wide[64 * ph : 64 * ph + 64, :], 1024, us)
    ):
        tg[64 * index : 64 * index + 64, :] = part
    back = mm(wc[0], tg[:, 512:1024]) + mm(wc[1], tg[:, 256:768]) + mm(wc[2], tg[:, 0:512])
    back = back.astype(BF16)
    for z in range(2):
        plane_rows = jnp.concatenate(
            [back[32 * ph : 32 * ph + 32, 256 * z : 256 * z + 256] for ph in range(4)], axis=1
        )
        igrads[z] = mm(plane_rows, order[...], nt).astype(BF16)


def reduce_kernel(samples, spaces, grads, out, slots_a, part, slots_b, sems):
    sample, space = lax.axis_index("sample"), lax.axis_index("space")
    size_a, size_b = group_sizes(samples, spaces)
    chunk_a = out.shape[0] // size_a
    chunk_b = chunk_a // size_b
    mine_a = sample * 4 + lax.rem(space, 4)
    mine_b = space // 4

    def peer_a(member):
        return (member // 4, mine_b * 4 + lax.rem(member, 4))

    def peer_b(member):
        return (sample, member * 4 + lax.rem(space, 4))

    others_a = [lax.rem(mine_a + d, size_a) for d in range(size_a)]
    others_b = [lax.rem(mine_b + d, size_b) for d in range(size_b)]
    barrier = pltpu.get_barrier_semaphore()
    for d in range(1, size_a):
        pl.semaphore_signal(barrier, inc=1, device_id=peer_a(others_a[d]), device_id_type=MESH)
    for d in range(1, size_b):
        pl.semaphore_signal(barrier, inc=1, device_id=peer_b(others_b[d]), device_id_type=MESH)
    pl.semaphore_wait(barrier, size_a + size_b - 2)

    def rows_a(member):
        return pl.ds(pl.multiple_of(member * chunk_a, 16), chunk_a)

    def rows_b(member):
        return pl.ds(pl.multiple_of(member * chunk_b, 16), chunk_b)

    def exchange(stage, count, make):
        copies = []
        for d in range(1, count):
            src, dst, target = make(d)
            copies.append(
                pltpu.make_async_remote_copy(
                    src_ref=src,
                    dst_ref=dst,
                    send_sem=sems.at[0, stage, d],
                    recv_sem=sems.at[1, stage, d],
                    device_id=target,
                    device_id_type=MESH,
                )
            )
        for item in copies:
            item.start()
        return copies

    def finish(copies):
        for item in copies:
            item.wait()

    finish(
        exchange(
            0,
            size_a,
            lambda d: (grads.at[rows_a(others_a[d])], slots_a.at[d], peer_a(others_a[d])),
        )
    )
    total = grads[rows_a(mine_a), :].astype(F32)
    for d in range(1, size_a):
        total += slots_a[d].astype(F32)
    part[...] = total.astype(BF16)
    finish(
        exchange(
            1,
            size_b,
            lambda d: (part.at[rows_b(others_b[d])], slots_b.at[d], peer_b(others_b[d])),
        )
    )
    total = part[rows_b(mine_b), :].astype(F32)
    for d in range(1, size_b):
        total += slots_b[d].astype(F32)
    here = pl.ds(pl.multiple_of(mine_a * chunk_a + mine_b * chunk_b, 16), chunk_b)
    out[here, :] = total.astype(BF16)
    finish(
        exchange(2, size_b, lambda d: (out.at[here], out.at[here], peer_b(others_b[d])))
    )
    whole = rows_a(mine_a)
    finish(
        exchange(3, size_a, lambda d: (out.at[whole], out.at[whole], peer_a(others_a[d])))
    )


def local(volume, out_grads, kernel_one, kernel_two):
    spaces, samples = lax.axis_size("space"), lax.axis_size("sample")
    depth, batch, channels_in, plane = volume.shape
    scale_one = float(samples * batch * spaces * depth * plane) ** (-0.5)
    scale_two = scale_one * 8.0**0.5
    vol = volume.reshape(depth, channels_in, plane)
    og = out_grads.reshape(128, 256)
    any_spec = pl.BlockSpec(memory_space=pl.ANY)
    vlo, vhi, olo, ohi = pl.pallas_call(
        functools.partial(halo_kernel, spaces),
        out_shape=[jax.ShapeDtypeStruct(a.shape, a.dtype) for a in (vol, vol, og, og)],
        in_specs=[any_spec] * 2,
        out_specs=[any_spec] * 4,
        scratch_shapes=[pltpu.SemaphoreType.DMA((4,)), pltpu.SemaphoreType.DMA((4,))],
        compiler_params=pltpu.CompilerParams(collective_id=0, has_side_effects=True),
        name="halo",
    )(vol, og)
    rows = padded_rows(samples, spaces)
    layer, igrads, grads = pl.pallas_call(
        functools.partial(math_kernel, spaces),
        out_shape=[
            jax.ShapeDtypeStruct((128, 256), BF16),
            jax.ShapeDtypeStruct((2, 32, 1024), BF16),
            jax.ShapeDtypeStruct((rows, 128), BF16),
        ],
        in_specs=[VMEM_SPEC] * 8,
        out_specs=[VMEM_SPEC] * 3,
        scratch_shapes=[
            pltpu.VMEM((1024, 1024), BF16),
            pltpu.VMEM((512, 1536), BF16),
            pltpu.VMEM((576, 768), BF16),
            pltpu.VMEM((512, 768), BF16),
            pltpu.VMEM((1024, 1024), BF16),
            pltpu.VMEM((3, 512, 256), BF16),
            pltpu.VMEM((3, 256, 512), BF16),
            pltpu.VMEM((3, 128, 1024), BF16),
            pltpu.VMEM((256, 1024), BF16),
        ],
        compiler_params=pltpu.CompilerParams(vmem_limit_bytes=48 * 2**20),
        name="conv_pair",
    )(vol, vlo, vhi, og, olo, ohi, kernel_one, kernel_two)
    size_a, size_b = group_sizes(samples, spaces)
    summed = pl.pallas_call(
        functools.partial(reduce_kernel, samples, spaces),
        out_shape=jax.ShapeDtypeStruct((rows, 128), BF16),
        in_specs=[VMEM_SPEC],
        out_specs=VMEM_SPEC,
        scratch_shapes=[
            pltpu.VMEM((size_a, rows // size_a, 128), BF16),
            pltpu.VMEM((rows // size_a, 128), BF16),
            pltpu.VMEM((size_b, rows // size_a // size_b, 128), BF16),
            pltpu.SemaphoreType.DMA((2, 4, max(size_a, size_b))),
        ],
        compiler_params=pltpu.CompilerParams(
            collective_id=1, has_side_effects=True, vmem_limit_bytes=32 * 2**20
        ),
        name="sum_all",
    )(grads)
    second = summed[:ROWS_TWO].reshape(27, 64, 128).astype(F32) * scale_two
    pair = summed[ROWS_TWO : ROWS_TWO + ROWS_ONE].reshape(PAIR, 32, 128)
    first = jnp.concatenate([pair[:, :, :64], pair[:-1, :, 64:]], axis=0).astype(F32) * scale_one
    return (
        layer.reshape(1, 1, 128, 256),
        igrads.reshape(volume.shape),
        first,
        second,
    )


def solution(mesh):
    in_specs = (P("space", "sample", None, None), P("space", "sample", None, None), P(), P())
    out_specs = (P("space", "sample", None, None), P("space", "sample", None, None), P(), P())
    return jax.shard_map(local, mesh=mesh, in_specs=in_specs, out_specs=out_specs, check_vma=False)
```

time: 336 us -> 51.8 us (0.15)
  local copies, waits for them, and re-layouts: 143 us -> 5.54 us
  waiting for transfers between devices: 128 us -> 0 us
  Pallas kernels: 0 us -> 43.1 us
  matrix products: 28.3 us -> 0 us
  starting transfers between devices: 17 us -> 0 us
  between operations: 15.2 us -> 0.71 us
    psum x1 -> x0, waiting for transfers between devices: 128 us -> none  [local(): first_grads = lax.psum(first_grads, ('sample', 'space'))]
    slice x34 -> x2, local copies, waits for them, and re-layouts: 125 us -> 0.11 us  [the longest x1 0.1 us: local(): pair[:-1, :, 64:]]
    pallas_call x0 -> x3, Pallas kernels: none -> 43.1 us  [the longest x1 32.6 us: local(): pl.pallas_call(functools.partial(reduce_kernel, samples, spaces), out_sha...]
    dot_general x54 -> x0, matrix products: 18.3 us -> none  [weight_grad(): jnp.einsum('zbiyx,zboyx->io', window, grads, preferred_element_type=jnp.f...]
    ppermute x6 -> x0, starting transfers between devices: 17 us -> none  [the longest x2 8.02 us: with_halo(): lax.ppermute(lax.slice_in_dim(block, block.shape[dim] - width, None, axis...]
    conv_general_dilated x4 -> x0, matrix products: 9.99 us -> none  [convolve(): lax.conv_general_dilated(inputs, kernel, (stride, stride, stride), margin...]
    conv_general_dilated x8 -> x0, local copies, waits for them, and re-layouts: 4.42 us -> none  [convolve(): lax.conv_general_dilated(inputs, kernel, (stride, stride, stride), margin...]
  transfers between devices with their start and end apart: 7 -> 0, of which waited for: 1 -> 0; matrix products, arithmetic and copies ran while one was open for 48% -> 0% of each run, Pallas kernels for 0% -> 0%
where the time goes in v1:
time: 51.8 us; the launch traced here: 51.2 us
  Pallas kernels  43.1 us (83%)
  local copies, waits for them, and re-layouts  5.54 us (11%)
  other arithmetic  1.8 us (3%)
  between operations  0.71 us (1%)
    pallas_call x1, Pallas kernels, local(): pl.pallas_call(functools.partial(reduce_kernel, samples, spaces), out_sha...  32.6 us
    pallas_call x1, Pallas kernels, local(): pl.pallas_call(functools.partial(math_kernel, spaces), out_shape=[jax.Sha...  6.09 us
    unnamed x16, local copies, waits for them, and re-layouts  5.44 us
    pallas_call x1, Pallas kernels, local(): pl.pallas_call(functools.partial(halo_kernel, spaces), out_shape=[jax.Sha...  4.43 us

profile of v1, /device:TPU:0, one launch (start us, length us, event | category | flops | bytes accessed | tf_op | source)
XLA Modules:
  0.0 51.2 jit_solution(17202147278148868323)
XLA Ops:
  0.6 0.0 copy-start
  0.6 0.0 copy-start.2
  0.7 4.4 %halo.1 = (bf16[2,32,1024]{2,1,0:T(8,128)(2,1)}, bf16[2,32,1024]{2,1,0:T(8,128)(2,1)}, bf16[128,256]{1,0:T(8,128)(2,1)}, bf16[128,256]{1,0:T(8,128)(2,1)}) custom-call(bf16[2,32,1024]{2,1,0:T(8,128)(2,1)} %bitcast.9, bf16[128,256]{1,0:T(8,128)(2,1)} %bitcast.11), custom_call_target="tpu_custom_call" | custom-call | tf_op jit(solution)/shard_map/halo/pallas_call | solution.py:333
  5.1 0.0 copy-done
  5.1 0.0 copy-done.2
  5.1 0.0 copy-start.1
  5.1 1.0 %copy-done.1 = bf16[27,64,128]{2,1,0:T(8,128)(2,1)S(1)} copy-done((bf16[27,64,128]{2,1,0:T(8,128)(2,1)S(1)}, bf16[27,64,128]{2,1,0:T(8,128)(2,1)}, u32[]{:S(2)}) %copy-start.1) | copy-done | bytes 442392
  6.1 0.0 copy-start.3
  6.1 0.9 %copy-done.3 = bf16[27,32,64]{2,1,0:T(8,128)(2,1)S(1)} copy-done((bf16[27,32,64]{2,1,0:T(8,128)(2,1)S(1)}, bf16[27,32,64]{2,1,0:T(8,128)(2,1)}, u32[]{:S(2)}) %copy-start.3) | copy-done | bytes 110616
  7.1 0.0 copy-start.4
  7.1 0.9 %copy-done.4 = bf16[2,32,1024]{2,1,0:T(8,128)(2,1)S(1)} copy-done((bf16[2,32,1024]{2,1,0:T(8,128)(2,1)S(1)}, bf16[2,32,1024]{2,1,0:T(8,128)(2,1)}, u32[]{:S(2)}) %copy-start.4) | copy-done | bytes 131096
  8.0 0.0 copy-start.5
  8.0 0.9 %copy-done.5 = bf16[2,32,1024]{2,1,0:T(8,128)(2,1)S(1)} copy-done((bf16[2,32,1024]{2,1,0:T(8,128)(2,1)S(1)}, bf16[2,32,1024]{2,1,0:T(8,128)(2,1)}, u32[]{:S(2)}) %copy-start.5) | copy-done | bytes 131096
  8.9 0.0 copy-start.6
  8.9 0.8 %copy-done.6 = bf16[128,256]{1,0:T(8,128)(2,1)S(1)} copy-done((bf16[128,256]{1,0:T(8,128)(2,1)S(1)}, bf16[128,256]{1,0:T(8,128)(2,1)}, u32[]{:S(2)}) %copy-start.6) | copy-done | bytes 65560
  9.7 0.0 copy-start.7
  9.7 0.8 %copy-done.7 = bf16[128,256]{1,0:T(8,128)(2,1)S(1)} copy-done((bf16[128,256]{1,0:T(8,128)(2,1)S(1)}, bf16[128,256]{1,0:T(8,128)(2,1)}, u32[]{:S(2)}) %copy-start.7) | copy-done | bytes 65560
  10.6 6.1 %conv_pair.1 = (bf16[128,256]{1,0:T(8,128)(2,1)}, bf16[2,32,1024]{2,1,0:T(8,128)(2,1)}, bf16[2560,128]{1,0:T(8,128)(2,1)S(1)}) custom-call(bf16[2,32,1024]{2,1,0:T(8,128)(2,1)S(1)} %bitcast.10, bf16[2,32,1024]{2,1,0:T(8,128)(2,1)S(1)} %copy-done.4, bf16[2,32,1024]{2,1,0:T(8,128)(2,1)S(1)} %copy-done.5, bf16[128,256]{1,0:T(8,128)(2,1)S(1)} %bitcast.12, ...), custom_call_target="tpu_custom_call" | custom-call | tf_op jit(solution)/shard_map/conv_pair/pallas_call | solution.py:343
  16.6 32.6 %sum_all.1 = bf16[2560,128]{1,0:T(8,128)(2,1)S(1)} custom-call(bf16[2560,128]{1,0:T(8,128)(2,1)S(1)} %get-tuple-element.17.grads), custom_call_target="tpu_custom_call" | custom-call | tf_op jit(solution)/shard_map/sum_all/pallas_call | solution.py:367
  49.2 0.1 slice.17
  49.3 0.8 %convert_multiply_fusion.1 = f32[27,32,64]{2,1,0:T(8,128)} fusion(bf16[13,32,64]{2,1,0:T(8,128)(2,1)S(1)} %slice.17, bf16[14,32,64]{2,1,0:T(8,128)(2,1)S(1)} %bitcast.14), kind=kLoop, calls=%fused_computation.1 | loop fusion | flops 165888 | bytes 331776 | tf_op jit(solution)/shard_map/mul | solution.py:385
  50.2 1.0 %convert_multiply_fusion = f32[1728,128]{1,0:T(8,128)} fusion(bf16[2560,128]{1,0:T(8,128)(2,1)S(1)} %sum_all.1), kind=kLoop, calls=%fused_computation | loop fusion | flops 442368 | bytes 1327104 | tf_op jit(solution)/shard_map/mul | solution.py:383
  (1 shorter events, 0.0 us)
Async XLA Ops:
  0.6 4.5 %copy-start = (bf16[2,1,32,1024]{3,2,1,0:T(8,128)(2,1)S(1)}, bf16[2,1,32,1024]{3,2,1,0:T(8,128)(2,1)}, u32[]{:S(2)}) copy-start(bf16[2,1,32,1024]{3,2,1,0:T(8,128)(2,1)} %param.4) | copy-start | bytes 393220
  0.6 4.5 %copy-start.2 = (bf16[1,1,128,256]{3,2,1,0:T(8,128)(2,1)S(1)}, bf16[1,1,128,256]{3,2,1,0:T(8,128)(2,1)}, u32[]{:S(2)}) copy-start(bf16[1,1,128,256]{3,2,1,0:T(8,128)(2,1)} %param.5) | copy-start | bytes 196612
  5.1 1.0 %copy-start.1 = (bf16[27,64,128]{2,1,0:T(8,128)(2,1)S(1)}, bf16[27,64,128]{2,1,0:T(8,128)(2,1)}, u32[]{:S(2)}) copy-start(bf16[27,64,128]{2,1,0:T(8,128)(2,1)} %k2.1) | copy-start | bytes 1327108
  6.1 0.9 %copy-start.3 = (bf16[27,32,64]{2,1,0:T(8,128)(2,1)S(1)}, bf16[27,32,64]{2,1,0:T(8,128)(2,1)}, u32[]{:S(2)}) copy-start(bf16[27,32,64]{2,1,0:T(8,128)(2,1)} %k1.1) | copy-start | bytes 331780
  7.1 0.9 %copy-start.4 = (bf16[2,32,1024]{2,1,0:T(8,128)(2,1)S(1)}, bf16[2,32,1024]{2,1,0:T(8,128)(2,1)}, u32[]{:S(2)}) copy-start(bf16[2,32,1024]{2,1,0:T(8,128)(2,1)} %get-tuple-element.11.vlo) | copy-start | bytes 393220
  8.0 0.9 %copy-start.5 = (bf16[2,32,1024]{2,1,0:T(8,128)(2,1)S(1)}, bf16[2,32,1024]{2,1,0:T(8,128)(2,1)}, u32[]{:S(2)}) copy-start(bf16[2,32,1024]{2,1,0:T(8,128)(2,1)} %get-tuple-element.12.vhi) | copy-start | bytes 393220
  8.9 0.8 %copy-start.6 = (bf16[128,256]{1,0:T(8,128)(2,1)S(1)}, bf16[128,256]{1,0:T(8,128)(2,1)}, u32[]{:S(2)}) copy-start(bf16[128,256]{1,0:T(8,128)(2,1)} %get-tuple-element.13.olo) | copy-start | bytes 196612
  9.7 0.8 %copy-start.7 = (bf16[128,256]{1,0:T(8,128)(2,1)S(1)}, bf16[128,256]{1,0:T(8,128)(2,1)}, u32[]{:S(2)}) copy-start(bf16[128,256]{1,0:T(8,128)(2,1)} %get-tuple-element.14.ohi) | copy-start | bytes 196612

commit v2 on v1

v2 whole, which is shorter than its diff:
```python
import functools

import jax
import jax.numpy as jnp
from jax import lax
from jax.experimental import pallas as pl
from jax.experimental.pallas import tpu as pltpu
from jax.sharding import PartitionSpec as P

F32 = jnp.float32
BF16 = jnp.bfloat16
MESH = pl.DeviceIdType.MESH
VMEM_SPEC = pl.BlockSpec(memory_space=pltpu.VMEM)
PAIR = 14
ROWS_TWO = 27 * 64
ROWS_ONE = PAIR * 32
WINDOWS = {-1: (1, -1), 0: (0, 0), 1: (1, 0), 2: (0, 1)}


def plan(samples, spaces):
    chips, lines = 2 * samples, spaces // 4
    unit = 2 * chips * 16
    rows = -(-(ROWS_TWO + ROWS_ONE) // unit) * unit
    early = ROWS_TWO // unit * unit
    return chips, lines, ((0, early), (early, rows - early))


def line_rows(size, chips, lines):
    return -(-(size // 2 // chips) // lines // 16) * 16


def mm(a, b, dims=((1,), (0,))):
    return lax.dot_general(a, b, (dims, ((), ())), preferred_element_type=F32)


def windows(parts, lanes, us):
    cell = lax.broadcasted_iota(jnp.int32, (1, lanes), 1)
    q, r = (cell >> 4) & 15, cell & 15
    for uy in us:
        for ux in us:
            (py, sy), (px, sx) = WINDOWS[uy], WINDOWS[ux]
            part = parts(2 * py + px)
            offset = 16 * sy + sx
            if offset != 0:
                part = pltpu.roll(part, (-offset) % lanes, 1)
                inside = (q + sy >= 0) & (q + sy <= 15) & (r + sx >= 0) & (r + sx <= 15)
                part = jnp.where(inside, part, 0.0)
            yield part.astype(BF16)


def tap_block(kernel, dz, dy, dx, shape):
    if 0 <= dy <= 2 and 0 <= dx <= 2:
        return kernel[9 * dz + 3 * dy + dx]
    return jnp.zeros(shape, BF16)


class Sum:
    def __init__(self, stream, base, size, samples, spaces, grads, out, bufs, sems):
        self.stream, self.base = stream, base
        self.grads, self.out, self.bufs, self.sems = grads, out, bufs, sems
        self.chips, self.lines = 2 * samples, spaces // 4
        sample, space = lax.axis_index("sample"), lax.axis_index("space")
        core, line = lax.rem(space, 2), space // 4
        chip = 2 * sample + lax.rem(space // 2, 2)
        self.core, self.chip, self.line = core, chip, line
        self.half = size // 2
        self.chunk = self.half // self.chips
        self.part = line_rows(size, self.chips, self.lines)
        self.sibling = (sample, space + 1 - 2 * core)
        self.others = [lax.rem(chip + d, self.chips) for d in range(self.chips)]
        self.chip_peers = [(c // 2, 4 * line + 2 * lax.rem(c, 2) + core) for c in self.others]
        self.ahead = [lax.rem(line + d, self.lines) for d in range(self.lines)]
        self.line_peers = [(sample, 4 * n + lax.rem(space, 4)) for n in self.ahead]
        self.flying = []

    def peers(self):
        return [self.sibling] + self.chip_peers[1:] + self.line_peers[1:]

    def rows(self, start, size):
        return pl.ds(pl.multiple_of(start, 16), size)

    def send(self, stage, items):
        self.flying = []
        for d, (src, dst, target) in enumerate(items):
            copy = pltpu.make_async_remote_copy(
                src_ref=src,
                dst_ref=dst,
                send_sem=self.sems.at[0, self.stream, stage, d],
                recv_sem=self.sems.at[1, self.stream, stage, d],
                device_id=target,
                device_id_type=MESH,
            )
            copy.start()
            self.flying.append(copy)

    def wait(self):
        for copy in self.flying:
            copy.wait()

    def pair(self):
        slot = self.bufs[0]
        away = self.rows(self.base + (1 - self.core) * self.half, self.half)
        self.send(0, [(self.grads.at[away], slot, self.sibling)])

    def plane(self):
        self.wait()
        slot, held, slots = self.bufs[0], self.bufs[1], self.bufs[2]
        own = self.grads[self.rows(self.base + self.core * self.half, self.half), :]
        held[...] = (own.astype(F32) + slot[...].astype(F32)).astype(BF16)
        items = []
        for d in range(1, self.chips):
            src = held.at[self.rows(self.others[d] * self.chunk, self.chunk)]
            items.append((src, slots.at[d], self.chip_peers[d]))
        self.send(1, items)

    def line_sum(self):
        self.wait()
        held, slots, part, far = self.bufs[1], self.bufs[2], self.bufs[3], self.bufs[4]
        total = held[self.rows(self.chip * self.chunk, self.chunk), :].astype(F32)
        for d in range(1, self.chips):
            total += slots[d].astype(F32)
        part[0 : self.chunk, :] = total.astype(BF16)
        extra = part.shape[0] - self.chunk
        if extra > 0:
            part[self.chunk :, :] = jnp.zeros((extra, 128), BF16)
        items = []
        for d in range(1, self.lines):
            src = part.at[self.rows(self.ahead[d] * self.part, self.part)]
            items.append((src, far.at[d], self.line_peers[d]))
        self.send(2, items)

    def line_back(self):
        self.wait()
        part, far, done = self.bufs[3], self.bufs[4], self.bufs[5]
        mine = self.rows(self.line * self.part, self.part)
        total = part[mine, :].astype(F32)
        for d in range(1, self.lines):
            total += far[d].astype(F32)
        done[mine, :] = total.astype(BF16)
        items = []
        for d in range(1, self.lines):
            items.append((done.at[mine], done.at[mine], self.line_peers[d]))
        self.send(3, items)

    def plane_back(self):
        self.wait()
        start = self.base + self.core * self.half + self.chip * self.chunk
        mine = self.rows(start, self.chunk)
        self.out[mine, :] = self.bufs[5][0 : self.chunk, :]
        items = []
        for d in range(1, self.chips):
            items.append((self.out.at[mine], self.out.at[mine], self.chip_peers[d]))
        self.send(4, items)

    def pair_back(self):
        self.wait()
        mine = self.rows(self.base + self.core * self.half, self.half)
        self.send(5, [(self.out.at[mine], self.out.at[mine], self.sibling)])


def whole_kernel(
    samples, spaces, vol_far, og_far, k1_far, k2_far,
    layer, igrads, out,
    vol, og, k1, k2, vlo, vhi, olo, ohi, grads,
    order, t1, t2, o4, tg, w1, wb, wc, hgrads,
    *rest,
):
    sems, local_sems, halo_sems = rest[12:]
    me, sample = lax.axis_index("space"), lax.axis_index("sample")
    has_low, has_high = me > 0, me < spaces - 1
    below, above = me - 1, me + 1
    fetched = [
        pltpu.make_async_copy(src, dst, local_sems.at[n])
        for n, (src, dst) in enumerate(
            [(k1_far, k1), (k2_far, k2), (vol_far, vol), (og_far, og)]
        )
    ]
    for item in fetched:
        item.start()

    _, _, streams = plan(samples, spaces)
    first, second = [
        Sum(n, base, size, samples, spaces, grads, out, rest[6 * n : 6 * n + 6], sems)
        for n, (base, size) in enumerate(streams)
    ]
    barrier = pltpu.get_barrier_semaphore()

    @pl.when(has_low)
    def _():
        pl.semaphore_signal(barrier, inc=1, device_id=(sample, below), device_id_type=MESH)

    @pl.when(has_high)
    def _():
        pl.semaphore_signal(barrier, inc=1, device_id=(sample, above), device_id_type=MESH)

    peers = first.peers()
    for peer in peers:
        pl.semaphore_signal(barrier, inc=1, device_id=peer, device_id_type=MESH)
    near = jnp.minimum(me, 1) + jnp.minimum(spaces - 1 - me, 1)
    pl.semaphore_wait(barrier, near + len(peers))

    def halo(src, dst, index, target):
        return pltpu.make_async_remote_copy(
            src_ref=src,
            dst_ref=dst,
            send_sem=halo_sems.at[0, index],
            recv_sem=halo_sems.at[1, index],
            device_id=(sample, target),
            device_id_type=MESH,
        )

    up = [(vol_far, vlo, 0), (og_far, olo, 1)]
    down = [(vol_far, vhi, 2), (og_far, ohi, 3)]

    @pl.when(has_high)
    def _():
        for src, dst, index in up:
            halo(src, dst, index, above).start()

    @pl.when(has_low)
    def _():
        for src, dst, index in down:
            halo(src, dst, index, below).start()

    def order_rows(step, carry):
        start = pl.multiple_of(step * 128, 128)
        col = lax.broadcasted_iota(jnp.int32, (1, 1024), 1)
        phase, q, r = col >> 8, (col >> 4) & 15, col & 15
        source = (2 * q + (phase >> 1)) * 32 + 2 * r + (phase & 1)
        row = lax.broadcasted_iota(jnp.int32, (128, 1024), 0) + start
        order[pl.ds(start, 128), :] = jnp.where(row == source, 1.0, 0.0).astype(BF16)
        return carry

    lax.fori_loop(0, 8, order_rows, 0)

    fetched[0].wait()
    fetched[1].wait()
    us = (-1, 0, 1, 2)
    phases = [(0, 0), (0, 1), (1, 0), (1, 1)]
    for dz in range(3):
        for index, (uy, ux) in enumerate((a, b) for a in us for b in us):
            w1[dz, 32 * index : 32 * index + 32, :] = jnp.concatenate(
                [tap_block(k1, dz, uy - py + 1, ux - px + 1, (32, 64)) for py, px in phases], axis=1
            )
        for index, (py, px) in enumerate(phases):
            wc[dz, 32 * index : 32 * index + 32, :] = jnp.concatenate(
                [tap_block(k1, dz, py + 1 - uy, px + 1 - ux, (32, 64)) for uy in us for ux in us],
                axis=1,
            )
            taps = {(0, 0): 1, (0, 1): -1, (1, 0): 2, (1, 1): 0}
            wb[dz, 64 * index : 64 * index + 64, :] = jnp.concatenate(
                [
                    tap_block(k2, dz, taps[py, sy], taps[px, sx], (64, 128))
                    for sy in (0, 1)
                    for sx in (0, 1)
                ],
                axis=1,
            )

    fetched[2].wait()
    fetched[3].wait()

    @pl.when(has_high)
    def _():
        for src, dst, index in up:
            halo(src, dst, index, above).wait_send()
        for src, dst, index in down:
            halo(src, dst, index, above).wait_recv()

    @pl.when(has_low)
    def _():
        for src, dst, index in down:
            halo(src, dst, index, below).wait_send()
        for src, dst, index in up:
            halo(src, dst, index, below).wait_recv()

    zero = jnp.zeros((), BF16)
    low = jnp.where(has_low, vlo[...].reshape(64, 1024), zero)
    high = jnp.where(has_high, vhi[...].reshape(64, 1024), zero)
    cells = jnp.concatenate([low, vol[...].reshape(64, 1024), high], axis=0)
    split = mm(cells, order[...])

    def volume_part(phase):
        return jnp.concatenate(
            [split[32 * p : 32 * p + 32, 256 * phase : 256 * phase + 256] for p in range(6)], axis=1
        )

    for index, part in enumerate(windows(volume_part, 1536, us)):
        t1[32 * index : 32 * index + 32, :] = part

    tn = ((0,), (0,))
    nt = ((1,), (1,))
    pre = mm(w1[0], t1[:, 0:1024], tn)
    pre += mm(w1[1], t1[:, 256:1280], tn)
    pre += mm(w1[2], t1[:, 512:1536], tn)
    sigma = 1.0 / (1.0 + jnp.exp(-pre))
    plane = lax.broadcasted_iota(jnp.int32, (1, 1024), 1) >> 8
    real = ((plane > 0) | has_low) & ((plane < 3) | has_high)
    hidden = jnp.where(real, pre * sigma, 0.0).astype(BF16).astype(F32)
    for index, part in enumerate(
        windows(lambda ph: hidden[64 * ph : 64 * ph + 64, 0:768], 768, (-1, 0, 1))
    ):
        t2[64 * index : 64 * index + 64, :] = part
    for dz in range(3):
        here = t2[:, 256 * dz : 256 * dz + 256]
        grads[576 * dz : 576 * dz + 576, :] = mm(here, og[...], nt).astype(BF16)
    first.pair()

    og_three = jnp.concatenate(
        [jnp.where(has_low, olo[...], zero), og[...], jnp.where(has_high, ohi[...], zero)], axis=1
    ).astype(F32)
    cell = lax.broadcasted_iota(jnp.int32, (1, 768), 1)
    q, r = (cell >> 4) & 15, cell & 15
    for sy in (0, 1):
        for sx in (0, 1):
            part = og_three
            if sy + sx > 0:
                part = pltpu.roll(part, 768 - 16 * sy - sx, 1)
                part = jnp.where((q + sy <= 15) & (r + sx <= 15), part, 0.0)
            index = 2 * sy + sx
            o4[128 * index : 128 * index + 128, :] = part.astype(BF16)

    even = mm(wb[1], o4[:, 256:768])
    odd = mm(wb[2], o4[:, 0:512]) + mm(wb[0], o4[:, 256:768])
    hgrads[:, 0:256] = odd[:, 0:256].astype(BF16)
    hgrads[:, 256:512] = even[:, 0:256].astype(BF16)
    hgrads[:, 512:768] = odd[:, 256:512].astype(BF16)
    hgrads[:, 768:1024] = even[:, 256:512].astype(BF16)

    slope = hgrads[...].astype(F32) * sigma * (1.0 + pre * (1.0 - sigma))
    pre_grads = jnp.where(real, slope, 0.0).astype(BF16)
    pre_wide = pre_grads.astype(F32)

    pairs = {}
    for dz in range(3):
        here = mm(t1[:, 256 * dz + 256 : 256 * dz + 768], pre_grads[:, 256:768], nt)
        for dy in range(3):
            for dx in range(3):
                term = None
                for index, (py, px) in enumerate(phases):
                    row = 32 * (4 * (py + dy) + px + dx)
                    block = here[row : row + 32, 64 * index : 64 * index + 64]
                    term = block if term is None else term + block
                pairs[9 * dz + 3 * dy + dx] = term
    pairs[27] = jnp.zeros((32, 64), F32)
    for tap in range(PAIR):
        grads[ROWS_TWO + 32 * tap : ROWS_TWO + 32 * tap + 32, :] = jnp.concatenate(
            [pairs[tap], pairs[tap + PAIR]], axis=1
        ).astype(BF16)
    used = ROWS_TWO + ROWS_ONE
    if grads.shape[0] > used:
        grads[used:, :] = jnp.zeros((grads.shape[0] - used, 128), BF16)
    second.pair()
    first.plane()

    total = jnp.zeros((128, 256), F32)
    for dz in range(3):
        here = t2[:, 256 * dz : 256 * dz + 256]
        total += mm(k2[9 * dz : 9 * dz + 9].reshape(576, 128), here, tn)
    layer[...] = total.astype(BF16)

    for index, part in enumerate(
        windows(lambda ph: pre_wide[64 * ph : 64 * ph + 64, :], 1024, us)
    ):
        tg[64 * index : 64 * index + 64, :] = part
    second.plane()

    back = mm(wc[0], tg[:, 512:1024]) + mm(wc[1], tg[:, 256:768]) + mm(wc[2], tg[:, 0:512])
    back = back.astype(BF16)
    for z in range(2):
        plane_rows = jnp.concatenate(
            [back[32 * ph : 32 * ph + 32, 256 * z : 256 * z + 256] for ph in range(4)], axis=1
        )
        igrads[z] = mm(plane_rows, order[...], nt).astype(BF16)

    first.line_sum()
    second.line_sum()
    first.line_back()
    second.line_back()
    first.plane_back()
    second.plane_back()
    first.pair_back()
    second.pair_back()
    first.wait()
    second.wait()


def local(volume, out_grads, kernel_one, kernel_two):
    spaces, samples = lax.axis_size("space"), lax.axis_size("sample")
    depth, batch, channels_in, plane = volume.shape
    scale_one = float(samples * batch * spaces * depth * plane) ** (-0.5)
    scale_two = scale_one * 8.0**0.5
    vol = volume.reshape(depth, channels_in, plane)
    og = out_grads.reshape(128, 256)
    chips, lines, streams = plan(samples, spaces)
    rows = streams[1][0] + streams[1][1]
    buffers = []
    for _, size in streams:
        half, chunk = size // 2, size // 2 // chips
        part = line_rows(size, chips, lines)
        buffers += [
            pltpu.VMEM((half, 128), BF16),
            pltpu.VMEM((half, 128), BF16),
            pltpu.VMEM((chips, chunk, 128), BF16),
            pltpu.VMEM((lines * part, 128), BF16),
            pltpu.VMEM((lines, part, 128), BF16),
            pltpu.VMEM((lines * part, 128), BF16),
        ]
    layer, igrads, summed = pl.pallas_call(
        functools.partial(whole_kernel, samples, spaces),
        out_shape=[
            jax.ShapeDtypeStruct((128, 256), BF16),
            jax.ShapeDtypeStruct((2, 32, 1024), BF16),
            jax.ShapeDtypeStruct((rows, 128), BF16),
        ],
        in_specs=[pl.BlockSpec(memory_space=pl.ANY)] * 4,
        out_specs=[VMEM_SPEC] * 3,
        scratch_shapes=[
            pltpu.VMEM(vol.shape, BF16),
            pltpu.VMEM(og.shape, BF16),
            pltpu.VMEM(kernel_one.shape, BF16),
            pltpu.VMEM(kernel_two.shape, BF16),
            pltpu.VMEM(vol.shape, BF16),
            pltpu.VMEM(vol.shape, BF16),
            pltpu.VMEM(og.shape, BF16),
            pltpu.VMEM(og.shape, BF16),
            pltpu.VMEM((rows, 128), BF16),
            pltpu.VMEM((1024, 1024), BF16),
            pltpu.VMEM((512, 1536), BF16),
            pltpu.VMEM((576, 768), BF16),
            pltpu.VMEM((512, 768), BF16),
            pltpu.VMEM((1024, 1024), BF16),
            pltpu.VMEM((3, 512, 256), BF16),
            pltpu.VMEM((3, 256, 512), BF16),
            pltpu.VMEM((3, 128, 1024), BF16),
            pltpu.VMEM((256, 1024), BF16),
            *buffers,
            pltpu.SemaphoreType.DMA((2, 2, 6, max(chips, lines))),
            pltpu.SemaphoreType.DMA((4,)),
            pltpu.SemaphoreType.DMA((2, 4)),
        ],
        compiler_params=pltpu.CompilerParams(
            collective_id=0, has_side_effects=True, vmem_limit_bytes=56 * 2**20
        ),
        name="conv_pair",
    )(vol, og, kernel_one, kernel_two)
    second = summed[:ROWS_TWO].reshape(27, 64, 128).astype(F32) * scale_two
    pair = summed[ROWS_TWO : ROWS_TWO + ROWS_ONE].reshape(PAIR, 32, 128)
    first = jnp.concatenate([pair[:, :, :64], pair[:-1, :, 64:]], axis=0).astype(F32) * scale_one
    return (
        layer.reshape(1, 1, 128, 256),
        igrads.reshape(volume.shape),
        first,
        second,
    )


def solution(mesh):
    in_specs = (P("space", "sample", None, None), P("space", "sample", None, None), P(), P())
    out_specs = (P("space", "sample", None, None), P("space", "sample", None, None), P(), P())
    return jax.shard_map(local, mesh=mesh, in_specs=in_specs, out_specs=out_specs, check_vma=False)
```

time: 51.8 us -> 40.2 us (0.78); the launches traced: 51.2 us -> 40.1 us
  Pallas kernels: 43.1 us -> 35 us
  local copies, waits for them, and re-layouts: 5.54 us -> 2.65 us
    pallas_call x3 -> x1, Pallas kernels: 43.1 us -> 35 us  [local(): pl.pallas_call(functools.partial(whole_kernel, samples, spaces), out_shap...]
    unnamed x16 -> x8, local copies, waits for them, and re-layouts: 5.44 us -> 1.59 us
    slice x1, local copies, waits for them, and re-layouts: 0.01 us -> 0.97 us  [local(): pair = summed[ROWS_TWO:ROWS_TWO + ROWS_ONE].reshape(PAIR, 32, 128)]
where the time goes in v2:
time: 40.2 us; the launch traced here: 40.1 us
  Pallas kernels  35 us (87%)
  local copies, waits for them, and re-layouts  2.65 us (7%)
  other arithmetic  1.8 us (4%)
  between operations  0.66 us (2%)
    pallas_call x1, Pallas kernels, local(): pl.pallas_call(functools.partial(whole_kernel, samples, spaces), out_shap...  35 us
    unnamed x8, local copies, waits for them, and re-layouts  1.59 us
    mul x1, other arithmetic, local(): second = summed[:ROWS_TWO].reshape(27, 64, 128).astype(F32) * scale_two  0.98 us
    slice x1, local copies, waits for them, and re-layouts, local(): pair = summed[ROWS_TWO:ROWS_TWO + ROWS_ONE].reshape(PAIR, 32, 128)  0.97 us
    mul x1, other arithmetic, local(): jnp.concatenate([pair[:, :, :64], pair[:-1, :, 64:]], axis=0).astype(F32)  0.82 us

profile of v2, /device:TPU:0, one launch (start us, length us, event | category | flops | bytes accessed | tf_op | source)
XLA Modules:
  0.0 40.1 jit_solution(1777438987811296572)
XLA Ops:
  0.6 35.0 %conv_pair.1 = (bf16[128,256]{1,0:T(8,128)(2,1)}, bf16[2,32,1024]{2,1,0:T(8,128)(2,1)}, bf16[2176,128]{1,0:T(8,128)(2,1)}) custom-call(bf16[2,32,1024]{2,1,0:T(8,128)(2,1)} %bitcast.13, bf16[128,256]{1,0:T(8,128)(2,1)} %bitcast.15, bf16[27,32,64]{2,1,0:T(8,128)(2,1)} %k1_far.1, bf16[27,64,128]{2,1,0:T(8,128)(2,1)} %k2_far.1), custom_call_target="tpu_custom_call" | custom-call | tf_op jit(solution)/shard_map/conv_pair/pallas_call | solution.py:409
  35.6 0.0 copy-start
  35.6 1.0 %slice.12 = bf16[448,128]{1,0:T(8,128)(2,1)S(1)} slice(bf16[2176,128]{1,0:T(8,128)(2,1)} %get-tuple-element.9), slice={[1728:2176], [0:128]} | slice | bytes 229376 | tf_op jit(solution)/shard_map/slice | solution.py:448
  36.6 0.1 slice.17
  36.7 0.8 %convert_multiply_fusion.1 = f32[27,32,64]{2,1,0:T(8,128)} fusion(bf16[13,32,64]{2,1,0:T(8,128)(2,1)S(1)} %slice.17, bf16[14,32,64]{2,1,0:T(8,128)(2,1)S(1)} %bitcast.10), kind=kLoop, calls=%fused_computation.1 | loop fusion | flops 165888 | bytes 331776 | tf_op jit(solution)/shard_map/mul | solution.py:449
  37.5 0.0 copy-done
  37.5 0.0 copy-start.2
  37.5 1.0 %convert_multiply_fusion = f32[1728,128]{1,0:T(8,128)} fusion(bf16[2176,128]{1,0:T(8,128)(2,1)S(1)} %copy-done), kind=kLoop, calls=%fused_computation | loop fusion | flops 442368 | bytes 1327104 | tf_op jit(solution)/shard_map/mul | solution.py:447
  38.5 0.0 copy-start.1
  38.5 0.0 copy-done.2
  38.5 0.6 %copy.11 = bf16[1,1,128,256]{3,2,1,0:T(8,128)(2,1)} copy(bf16[1,1,128,256]{3,2,1,0:T(8,128)(2,1)S(1)} %bitcast.14) | data formatting | bytes 131072
  39.1 0.3 copy-done.1
  39.4 0.7 %copy.12 = bf16[2,1,32,1024]{3,2,1,0:T(8,128)(2,1)} copy(bf16[2,1,32,1024]{3,2,1,0:T(8,128)(2,1)S(1)} %bitcast.12) | data formatting | bytes 262144
Async XLA Ops:
  35.6 1.9 %copy-start = (bf16[2176,128]{1,0:T(8,128)(2,1)S(1)}, bf16[2176,128]{1,0:T(8,128)(2,1)}, u32[]{:S(2)}) copy-start(bf16[2176,128]{1,0:T(8,128)(2,1)} %get-tuple-element.9) | copy-start | bytes 1671172
  37.5 1.0 %copy-start.2 = (bf16[128,256]{1,0:T(8,128)(2,1)S(1)}, bf16[128,256]{1,0:T(8,128)(2,1)}, u32[]{:S(2)}) copy-start(bf16[128,256]{1,0:T(8,128)(2,1)} %get-tuple-element.7) | copy-start | bytes 196612
  38.5 0.9 %copy-start.1 = (bf16[2,32,1024]{2,1,0:T(8,128)(2,1)S(1)}, bf16[2,32,1024]{2,1,0:T(8,128)(2,1)}, u32[]{:S(2)}) copy-start(bf16[2,32,1024]{2,1,0:T(8,128)(2,1)} %get-tuple-element.8) | copy-start | bytes 393220

commit v3 on v2

--- a/solution.py
+++ b/solution.py
@@ -55,8 +55,8 @@
 
 
 class Sum:
-    def __init__(self, stream, base, size, samples, spaces, grads, out, bufs, sems):
-        self.stream, self.base = stream, base
+    def __init__(self, base, size, samples, spaces, grads, out, bufs, sems):
+        self.base = base
         self.grads, self.out, self.bufs, self.sems = grads, out, bufs, sems
         self.chips, self.lines = 2 * samples, spaces // 4
         sample, space = lax.axis_index("sample"), lax.axis_index("space")
@@ -73,9 +73,6 @@
         self.line_peers = [(sample, 4 * n + lax.rem(space, 4)) for n in self.ahead]
         self.flying = []
 
-    def peers(self):
-        return [self.sibling] + self.chip_peers[1:] + self.line_peers[1:]
-
     def rows(self, start, size):
         return pl.ds(pl.multiple_of(start, 16), size)
 
@@ -85,8 +82,8 @@
             copy = pltpu.make_async_remote_copy(
                 src_ref=src,
                 dst_ref=dst,
-                send_sem=self.sems.at[0, self.stream, stage, d],
-                recv_sem=self.sems.at[1, self.stream, stage, d],
+                send_sem=self.sems.at[0, stage, d],
+                recv_sem=self.sems.at[1, stage, d],
                 device_id=target,
                 device_id_type=MESH,
             )
@@ -158,6 +155,66 @@
         self.send(5, [(self.out.at[mine], self.out.at[mine], self.sibling)])
 
 
+class QuickSum:
+    def __init__(self, first, base, size, grads, out, bufs, sems):
+        self.first, self.base, self.grads, self.out, self.bufs = first, base, grads, out, bufs
+        self.sems = sems
+        self.members = 2 * first.chips
+        self.chunk = size // self.members
+        me = 2 * first.chip + first.core
+        self.mine = first.rows(base + me * self.chunk, self.chunk)
+        self.others = [lax.rem(me + d, self.members) for d in range(self.members)]
+        self.peers = [
+            (m // 4, 4 * first.line + 2 * lax.rem(m // 2, 2) + lax.rem(m, 2)) for m in self.others
+        ]
+
+    def send(self, stage, items):
+        self.flying = []
+        for d, (src, dst, target) in enumerate(items):
+            copy = pltpu.make_async_remote_copy(
+                src_ref=src,
+                dst_ref=dst,
+                send_sem=self.sems.at[0, stage, d],
+                recv_sem=self.sems.at[1, stage, d],
+                device_id=target,
+                device_id_type=MESH,
+            )
+            copy.start()
+            self.flying.append(copy)
+
+    def wait(self):
+        for copy in self.flying:
+            copy.wait()
+
+    def plane(self):
+        items = []
+        for d in range(1, self.members):
+            away = self.first.rows(self.base + self.others[d] * self.chunk, self.chunk)
+            items.append((self.grads.at[away], self.bufs[0].at[d], self.peers[d]))
+        self.send(0, items)
+
+    def line(self):
+        self.wait()
+        slots, held = self.bufs
+        total = self.grads[self.mine, :].astype(F32)
+        for d in range(1, self.members):
+            total += slots[d].astype(F32)
+        here = self.first.rows(self.first.line * self.chunk, self.chunk)
+        held[here, :] = total.astype(BF16)
+        target = held.at[here]
+        self.send(1, [(target, target, peer) for peer in self.first.line_peers[1:]])
+
+    def back(self):
+        self.wait()
+        held = self.bufs[1]
+        total = held[0 : self.chunk, :].astype(F32)
+        for n in range(1, self.first.lines):
+            total += held[n * self.chunk : (n + 1) * self.chunk, :].astype(F32)
+        self.out[self.mine, :] = total.astype(BF16)
+        target = self.out.at[self.mine]
+        self.send(2, [(target, target, peer) for peer in self.peers[1:]])
+
+
 def whole_kernel(
     samples, spaces, vol_far, og_far, k1_far, k2_far,
     layer, igrads, out,
@@ -165,7 +222,7 @@
     order, t1, t2, o4, tg, w1, wb, wc, hgrads,
     *rest,
 ):
-    sems, local_sems, halo_sems = rest[12:]
+    sems, quick_sems, local_sems, halo_sems = rest[8:]
     me, sample = lax.axis_index("space"), lax.axis_index("sample")
     has_low, has_high = me > 0, me < spaces - 1
     below, above = me - 1, me + 1
@@ -179,10 +236,8 @@
         item.start()
 
     _, _, streams = plan(samples, spaces)
-    first, second = [
-        Sum(n, base, size, samples, spaces, grads, out, rest[6 * n : 6 * n + 6], sems)
-        for n, (base, size) in enumerate(streams)
-    ]
+    first = Sum(*streams[0], samples, spaces, grads, out, rest[0:6], sems)
+    second = QuickSum(first, *streams[1], grads, out, rest[6:8], quick_sems)
     barrier = pltpu.get_barrier_semaphore()
 
     @pl.when(has_low)
@@ -193,7 +248,7 @@
     def _():
         pl.semaphore_signal(barrier, inc=1, device_id=(sample, above), device_id_type=MESH)
 
-    peers = first.peers()
+    peers = second.peers[1:] + first.line_peers[1:]
     for peer in peers:
         pl.semaphore_signal(barrier, inc=1, device_id=peer, device_id_type=MESH)
     near = jnp.minimum(me, 1) + jnp.minimum(spaces - 1 - me, 1)
@@ -209,8 +264,8 @@
             device_id_type=MESH,
         )
 
-    up = [(vol_far, vlo, 0), (og_far, olo, 1)]
-    down = [(vol_far, vhi, 2), (og_far, ohi, 3)]
+    up = [(og_far, olo, 0), (vol_far, vlo, 1)]
+    down = [(og_far, ohi, 2), (vol_far, vhi, 3)]
 
     @pl.when(has_high)
     def _():
@@ -257,24 +312,46 @@
                 axis=1,
             )
 
+    def arrive(n):
+        @pl.when(has_high)
+        def _():
+            src, dst, index = up[n]
+            halo(src, dst, index, above).wait_send()
+            src, dst, index = down[n]
+            halo(src, dst, index, above).wait_recv()
+
+        @pl.when(has_low)
+        def _():
+            src, dst, index = down[n]
+            halo(src, dst, index, below).wait_send()
+            src, dst, index = up[n]
+            halo(src, dst, index, below).wait_recv()
+
     fetched[2].wait()
     fetched[3].wait()
-
-    @pl.when(has_high)
-    def _():
-        for src, dst, index in up:
-            halo(src, dst, index, above).wait_send()
-        for src, dst, index in down:
-            halo(src, dst, index, above).wait_recv()
-
-    @pl.when(has_low)
-    def _():
-        for src, dst, index in down:
-            halo(src, dst, index, below).wait_send()
-        for src, dst, index in up:
-            halo(src, dst, index, below).wait_recv()
-
+    arrive(0)
     zero = jnp.zeros((), BF16)
+    og_three = jnp.concatenate(
+        [jnp.where(has_low, olo[...], zero), og[...], jnp.where(has_high, ohi[...], zero)], axis=1
+    ).astype(F32)
+    cell = lax.broadcasted_iota(jnp.int32, (1, 768), 1)
+    q, r = (cell >> 4) & 15, cell & 15
+    for sy in (0, 1):
+        for sx in (0, 1):
+            part = og_three
+            if sy + sx > 0:
+                part = pltpu.roll(part, 768 - 16 * sy - sx, 1)
+                part = jnp.where((q + sy <= 15) & (r + sx <= 15), part, 0.0)
+            index = 2 * sy + sx
+            o4[128 * index : 128 * index + 128, :] = part.astype(BF16)
+
+    even = mm(wb[1], o4[:, 256:768])
+    odd = mm(wb[2], o4[:, 0:512]) + mm(wb[0], o4[:, 256:768])
+    hgrads[:, 0:256] = odd[:, 0:256].astype(BF16)
+    hgrads[:, 256:512] = even[:, 0:256].astype(BF16)
+    hgrads[:, 512:768] = odd[:, 256:512].astype(BF16)
+    hgrads[:, 768:1024] = even[:, 256:512].astype(BF16)
+    arrive(1)
     low = jnp.where(has_low, vlo[...].reshape(64, 1024), zero)
     high = jnp.where(has_high, vhi[...].reshape(64, 1024), zero)
     cells = jnp.concatenate([low, vol[...].reshape(64, 1024), high], axis=0)
@@ -306,30 +383,17 @@
         grads[576 * dz : 576 * dz + 576, :] = mm(here, og[...], nt).astype(BF16)
     first.pair()
 
-    og_three = jnp.concatenate(
-        [jnp.where(has_low, olo[...], zero), og[...], jnp.where(has_high, ohi[...], zero)], axis=1
-    ).astype(F32)
-    cell = lax.broadcasted_iota(jnp.int32, (1, 768), 1)
-    q, r = (cell >> 4) & 15, cell & 15
-    for sy in (0, 1):
-        for sx in (0, 1):
-            part = og_three
-            if sy + sx > 0:
-                part = pltpu.roll(part, 768 - 16 * sy - sx, 1)
-                part = jnp.where((q + sy <= 15) & (r + sx <= 15), part, 0.0)
-            index = 2 * sy + sx
-            o4[128 * index : 128 * index + 128, :] = part.astype(BF16)
-
-    even = mm(wb[1], o4[:, 256:768])
-    odd = mm(wb[2], o4[:, 0:512]) + mm(wb[0], o4[:, 256:768])
-    hgrads[:, 0:256] = odd[:, 0:256].astype(BF16)
-    hgrads[:, 256:512] = even[:, 0:256].astype(BF16)
-    hgrads[:, 512:768] = odd[:, 256:512].astype(BF16)
-    hgrads[:, 768:1024] = even[:, 256:512].astype(BF16)
+    total = jnp.zeros((128, 256), F32)
+    for dz in range(3):
+        here = t2[:, 256 * dz : 256 * dz + 256]
+        total += mm(k2[9 * dz : 9 * dz + 9].reshape(576, 128), here, tn)
+    layer[...] = total.astype(BF16)
 
     slope = hgrads[...].astype(F32) * sigma * (1.0 + pre * (1.0 - sigma))
     pre_grads = jnp.where(real, slope, 0.0).astype(BF16)
     pre_wide = pre_grads.astype(F32)
+
+    first.plane()
 
     pairs = {}
     for dz in range(3):
@@ -350,21 +414,12 @@
     used = ROWS_TWO + ROWS_ONE
     if grads.shape[0] > used:
         grads[used:, :] = jnp.zeros((grads.shape[0] - used, 128), BF16)
-    second.pair()
-    first.plane()
-
-    total = jnp.zeros((128, 256), F32)
-    for dz in range(3):
-        here = t2[:, 256 * dz : 256 * dz + 256]
-        total += mm(k2[9 * dz : 9 * dz + 9].reshape(576, 128), here, tn)
-    layer[...] = total.astype(BF16)
+    second.plane()
 
     for index, part in enumerate(
         windows(lambda ph: pre_wide[64 * ph : 64 * ph + 64, :], 1024, us)
     ):
         tg[64 * index : 64 * index + 64, :] = part
-    second.plane()
-
     back = mm(wc[0], tg[:, 512:1024]) + mm(wc[1], tg[:, 256:768]) + mm(wc[2], tg[:, 0:512])
     back = back.astype(BF16)
     for z in range(2):
@@ -374,15 +429,24 @@
         igrads[z] = mm(plane_rows, order[...], nt).astype(BF16)
 
     first.line_sum()
-    second.line_sum()
+    second.line()
     first.line_back()
-    second.line_back()
+    second.back()
     first.plane_back()
-    second.plane_back()
     first.pair_back()
-    second.pair_back()
+    second.wait()
     first.wait()
-    second.wait()
+
+
+def tail_kernel(scale_one, scale_two, layer, igrads, summed, layer_out, igrads_out, first, second):
+    layer_out[...] = layer[...]
+    igrads_out[...] = igrads[...]
+    second[...] = summed[0:ROWS_TWO, :].astype(F32) * scale_two
+    for tap in range(27):
+        start = ROWS_TWO + 32 * (tap % PAIR)
+        block = summed[start : start + 32, :]
+        half = block[:, 0:64] if tap < PAIR else block[:, 64:128]
+        first[tap] = half.astype(F32) * scale_one
 
 
 def local(volume, out_grads, kernel_one, kernel_two):
@@ -394,18 +458,9 @@
     og = out_grads.reshape(128, 256)
     chips, lines, streams = plan(samples, spaces)
     rows = streams[1][0] + streams[1][1]
-    buffers = []
-    for _, size in streams:
-        half, chunk = size // 2, size // 2 // chips
-        part = line_rows(size, chips, lines)
-        buffers += [
-            pltpu.VMEM((half, 128), BF16),
-            pltpu.VMEM((half, 128), BF16),
-            pltpu.VMEM((chips, chunk, 128), BF16),
-            pltpu.VMEM((lines * part, 128), BF16),
-            pltpu.VMEM((lines, part, 128), BF16),
-            pltpu.VMEM((lines * part, 128), BF16),
-        ]
+    early, late = streams[0][1], streams[1][1]
+    half, chunk = early // 2, early // 2 // chips
+    part, quick = line_rows(early, chips, lines), late // 2 // chips
     layer, igrads, summed = pl.pallas_call(
         functools.partial(whole_kernel, samples, spaces),
         out_shape=[
@@ -413,7 +468,7 @@
             jax.ShapeDtypeStruct((2, 32, 1024), BF16),
             jax.ShapeDtypeStruct((rows, 128), BF16),
         ],
-        in_specs=[pl.BlockSpec(memory_space=pl.ANY)] * 4,
+        in_specs=[pl.BlockSpec(memory_space=pltpu.HBM)] * 4,
         out_specs=[VMEM_SPEC] * 3,
         scratch_shapes=[
             pltpu.VMEM(vol.shape, BF16),
@@ -434,8 +489,16 @@
             pltpu.VMEM((3, 256, 512), BF16),
             pltpu.VMEM((3, 128, 1024), BF16),
             pltpu.VMEM((256, 1024), BF16),
-            *buffers,
-            pltpu.SemaphoreType.DMA((2, 2, 6, max(chips, lines))),
+            pltpu.VMEM((half, 128), BF16),
+            pltpu.VMEM((half, 128), BF16),
+            pltpu.VMEM((chips, chunk, 128), BF16),
+            pltpu.VMEM((lines * part, 128), BF16),
+            pltpu.VMEM((lines, part, 128), BF16),
+            pltpu.VMEM((lines * part, 128), BF16),
+            pltpu.VMEM((2 * chips, quick, 128), BF16),
+            pltpu.VMEM((lines * quick, 128), BF16),
+            pltpu.SemaphoreType.DMA((2, 6, max(chips, lines))),
+            pltpu.SemaphoreType.DMA((2, 3, max(2 * chips, lines))),
             pltpu.SemaphoreType.DMA((4,)),
             pltpu.SemaphoreType.DMA((2, 4)),
         ],
@@ -444,14 +507,24 @@
         ),
         name="conv_pair",
     )(vol, og, kernel_one, kernel_two)
-    second = summed[:ROWS_TWO].reshape(27, 64, 128).astype(F32) * scale_two
-    pair = summed[ROWS_TWO : ROWS_TWO + ROWS_ONE].reshape(PAIR, 32, 128)
-    first = jnp.concatenate([pair[:, :, :64], pair[:-1, :, 64:]], axis=0).astype(F32) * scale_one
+    layer, igrads, first, second = pl.pallas_call(
+        functools.partial(tail_kernel, scale_one, scale_two),
+        out_shape=[
+            jax.ShapeDtypeStruct(layer.shape, BF16),
+            jax.ShapeDtypeStruct(igrads.shape, BF16),
+            jax.ShapeDtypeStruct(kernel_one.shape, F32),
+            jax.ShapeDtypeStruct((ROWS_TWO, 128), F32),
+        ],
+        in_specs=[VMEM_SPEC] * 3,
+        out_specs=[VMEM_SPEC] * 4,
+        compiler_params=pltpu.CompilerParams(vmem_limit_bytes=56 * 2**20),
+        name="finish",
+    )(layer, igrads, summed)
     return (
-        layer.reshape(1, 1, 128, 256),
+        layer.reshape(out_grads.shape),
         igrads.reshape(volume.shape),
         first,
-        second,
+        second.reshape(kernel_two.shape),
     )
 
 

time: 40.2 us -> 39.8 us (0.990)
  Pallas kernels: 35 us -> 39 us
  local copies, waits for them, and re-layouts: 2.65 us -> 0 us
  other arithmetic: 1.8 us -> 0 us
    pallas_call x0 -> x1, Pallas kernels: none -> 2.37 us  [local(): pl.pallas_call(functools.partial(tail_kernel, scale_one, scale_two), out_...]
    mul x2 -> x0, other arithmetic: 1.8 us -> none  [the longest x1 0.98 us: local(): second = summed[:ROWS_TWO].reshape(27, 64, 128).astype(F32) * scale_two]
    pallas_call x1, Pallas kernels: 35 us -> 36.6 us  [local(): pl.pallas_call(functools.partial(whole_kernel, samples, spaces), out_shap...]
    unnamed x8 -> x0, local copies, waits for them, and re-layouts: 1.59 us -> none
    slice x2 -> x0, local copies, waits for them, and re-layouts: 1.07 us -> none  [the longest x1 0.97 us: local(): pair = summed[ROWS_TWO:ROWS_TWO + ROWS_ONE].reshape(PAIR, 32, 128)]
where the time goes in v3:
time: 39.8 us; the launch traced here: 39.6 us
  Pallas kernels  39 us (98%)
  between operations  0.64 us (2%)
    pallas_call x1, Pallas kernels, local(): pl.pallas_call(functools.partial(whole_kernel, samples, spaces), out_shap...  36.6 us
    pallas_call x1, Pallas kernels, local(): pl.pallas_call(functools.partial(tail_kernel, scale_one, scale_two), out_...  2.37 us

profile of v3, /device:TPU:0, one launch (start us, length us, event | category | flops | bytes accessed | tf_op | source)
XLA Modules:
  0.0 39.6 jit_solution(7496415498116025665)
XLA Ops:
  0.6 36.6 %conv_pair.1 = (bf16[128,256]{1,0:T(8,128)(2,1)}, bf16[2,32,1024]{2,1,0:T(8,128)(2,1)}, bf16[2176,128]{1,0:T(8,128)(2,1)}) custom-call(bf16[2,32,1024]{2,1,0:T(8,128)(2,1)} %bitcast.7, bf16[128,256]{1,0:T(8,128)(2,1)} %bitcast.8, bf16[27,32,64]{2,1,0:T(8,128)(2,1)} %k1_far.1, bf16[27,64,128]{2,1,0:T(8,128)(2,1)} %k2_far.1), custom_call_target="tpu_custom_call" | custom-call | tf_op jit(solution)/shard_map/conv_pair/pallas_call | solution.py:464
  37.2 2.4 %finish.1 = (bf16[128,256]{1,0:T(8,128)(2,1)}, bf16[2,32,1024]{2,1,0:T(8,128)(2,1)}, f32[27,32,64]{2,1,0:T(8,128)}, f32[1728,128]{1,0:T(8,128)}) custom-call(bf16[128,256]{1,0:T(8,128)(2,1)} %get-tuple-element.11.layer, bf16[2,32,1024]{2,1,0:T(8,128)(2,1)} %get-tuple-element.12.igrads, bf16[2176,128]{1,0:T(8,128)(2,1)} %get-tuple-element.13.summed), custom_call_target="tpu_custom_call" | custom-call | tf_op jit(solution)/shard_map/finish/pallas_call | solution.py:510

commit v4 on v3

--- a/solution.py
+++ b/solution.py
@@ -1,4 +1,5 @@
 import functools
+import math
 
 import jax
 import jax.numpy as jnp
@@ -19,14 +20,18 @@
 
 def plan(samples, spaces):
     chips, lines = 2 * samples, spaces // 4
-    unit = 2 * chips * 16
-    rows = -(-(ROWS_TWO + ROWS_ONE) // unit) * unit
-    early = ROWS_TWO // unit * unit
-    return chips, lines, ((0, early), (early, rows - early))
-
-
-def line_rows(size, chips, lines):
-    return -(-(size // 2 // chips) // lines // 16) * 16
+    unit = 32 * math.lcm(chips, lines)
+    units = -(-(ROWS_TWO + ROWS_ONE) // unit)
+    early = ROWS_TWO // unit
+    cut = (early + 1) // 2
+    bounds = [0, cut * unit, early * unit, units * unit]
+    streams = [(bounds[n], bounds[n + 1] - bounds[n], n == 1) for n in range(3)]
+    return chips, lines, streams
+
+
+def level_rows(size, outer, inner):
+    chunk = size // 2 // outer
+    return chunk, -(-chunk // inner // 16) * 16
 
 
 def mm(a, b, dims=((1,), (0,))):
@@ -55,23 +60,25 @@
 
 
 class Sum:
-    def __init__(self, base, size, samples, spaces, grads, out, bufs, sems):
-        self.base = base
-        self.grads, self.out, self.bufs, self.sems = grads, out, bufs, sems
-        self.chips, self.lines = 2 * samples, spaces // 4
+    def __init__(self, stream, samples, spaces, grads, out, bufs, sems):
+        self.base, size, line_first = stream
+        self.grads, self.out, self.sems = grads, out, sems
+        self.slot, self.held, self.slots, self.part, self.far, self.done = bufs
+        chips, lines = 2 * samples, spaces // 4
         sample, space = lax.axis_index("sample"), lax.axis_index("space")
         core, line = lax.rem(space, 2), space // 4
         chip = 2 * sample + lax.rem(space // 2, 2)
-        self.core, self.chip, self.line = core, chip, line
-        self.half = size // 2
-        self.chunk = self.half // self.chips
-        self.part = line_rows(size, self.chips, self.lines)
+        self.core, self.half = core, size // 2
         self.sibling = (sample, space + 1 - 2 * core)
-        self.others = [lax.rem(chip + d, self.chips) for d in range(self.chips)]
-        self.chip_peers = [(c // 2, 4 * line + 2 * lax.rem(c, 2) + core) for c in self.others]
-        self.ahead = [lax.rem(line + d, self.lines) for d in range(self.lines)]
-        self.line_peers = [(sample, 4 * n + lax.rem(space, 4)) for n in self.ahead]
-        self.flying = []
+        others = [lax.rem(chip + d, chips) for d in range(chips)]
+        ahead = [lax.rem(line + d, lines) for d in range(lines)]
+        plane = (chip, others, [(c // 2, 4 * line + 2 * lax.rem(c, 2) + core) for c in others])
+        column = (line, ahead, [(sample, 4 * n + lax.rem(space, 4)) for n in ahead])
+        self.outer, self.inner = (column, plane) if line_first else (plane, column)
+        self.chunk, self.piece = level_rows(size, len(self.outer[1]), len(self.inner[1]))
+
+    def peers(self):
+        return [self.sibling] + self.outer[2][1:] + self.inner[2][1:]
 
     def rows(self, start, size):
         return pl.ds(pl.multiple_of(start, 16), size)
@@ -94,125 +101,57 @@
         for copy in self.flying:
             copy.wait()
 
+    def scatter(self, stage, level, source, size, slots):
+        _, indices, peers = level
+        items = []
+        for d in range(1, len(peers)):
+            src = source.at[self.rows(indices[d] * size, size)]
+            items.append((src, slots.at[d], peers[d]))
+        self.send(stage, items)
+
+    def gathered(self, level, source, size, slots):
+        total = source[self.rows(level[0] * size, size), :].astype(F32)
+        for d in range(1, len(level[2])):
+            total += slots[d].astype(F32)
+        return total.astype(BF16)
+
     def pair(self):
-        slot = self.bufs[0]
         away = self.rows(self.base + (1 - self.core) * self.half, self.half)
-        self.send(0, [(self.grads.at[away], slot, self.sibling)])
-
-    def plane(self):
+        self.send(0, [(self.grads.at[away], self.slot, self.sibling)])
+
+    def first_level(self):
         self.wait()
-        slot, held, slots = self.bufs[0], self.bufs[1], self.bufs[2]
         own = self.grads[self.rows(self.base + self.core * self.half, self.half), :]
-        held[...] = (own.astype(F32) + slot[...].astype(F32)).astype(BF16)
-        items = []
-        for d in range(1, self.chips):
-            src = held.at[self.rows(self.others[d] * self.chunk, self.chunk)]
-            items.append((src, slots.at[d], self.chip_peers[d]))
-        self.send(1, items)
-
-    def line_sum(self):
+        self.held[...] = (own.astype(F32) + self.slot[...].astype(F32)).astype(BF16)
+        self.scatter(1, self.outer, self.held, self.chunk, self.slots)
+
+    def second_level(self):
         self.wait()
-        held, slots, part, far = self.bufs[1], self.bufs[2], self.bufs[3], self.bufs[4]
-        total = held[self.rows(self.chip * self.chunk, self.chunk), :].astype(F32)
-        for d in range(1, self.chips):
-            total += slots[d].astype(F32)
-        part[0 : self.chunk, :] = total.astype(BF16)
-        extra = part.shape[0] - self.chunk
+        self.part[0 : self.chunk, :] = self.gathered(self.outer, self.held, self.chunk, self.slots)
+        extra = self.part.shape[0] - self.chunk
         if extra > 0:
-            part[self.chunk :, :] = jnp.zeros((extra, 128), BF16)
-        items = []
-        for d in range(1, self.lines):
-            src = part.at[self.rows(self.ahead[d] * self.part, self.part)]
-            items.append((src, far.at[d], self.line_peers[d]))
-        self.send(2, items)
-
-    def line_back(self):
+            self.part[self.chunk :, :] = jnp.zeros((extra, 128), BF16)
+        self.scatter(2, self.inner, self.part, self.piece, self.far)
+
+    def second_back(self):
         self.wait()
-        part, far, done = self.bufs[3], self.bufs[4], self.bufs[5]
-        mine = self.rows(self.line * self.part, self.part)
-        total = part[mine, :].astype(F32)
-        for d in range(1, self.lines):
-            total += far[d].astype(F32)
-        done[mine, :] = total.astype(BF16)
-        items = []
-        for d in range(1, self.lines):
-            items.append((done.at[mine], done.at[mine], self.line_peers[d]))
-        self.send(3, items)
-
-    def plane_back(self):
+        mine = self.rows(self.inner[0] * self.piece, self.piece)
+        self.done[mine, :] = self.gathered(self.inner, self.part, self.piece, self.far)
+        target = self.done.at[mine]
+        self.send(3, [(target, target, peer) for peer in self.inner[2][1:]])
+
+    def first_back(self):
         self.wait()
-        start = self.base + self.core * self.half + self.chip * self.chunk
+        start = self.base + self.core * self.half + self.outer[0] * self.chunk
         mine = self.rows(start, self.chunk)
-        self.out[mine, :] = self.bufs[5][0 : self.chunk, :]
-        items = []
-        for d in range(1, self.chips):
-            items.append((self.out.at[mine], self.out.at[mine], self.chip_peers[d]))
-        self.send(4, items)
+        self.out[mine, :] = self.done[0 : self.chunk, :]
+        target = self.out.at[mine]
+        self.send(4, [(target, target, peer) for peer in self.outer[2][1:]])
 
     def pair_back(self):
         self.wait()
-        mine = self.rows(self.base + self.core * self.half, self.half)
-        self.send(5, [(self.out.at[mine], self.out.at[mine], self.sibling)])
-
-
-class QuickSum:
-    def __init__(self, first, base, size, grads, out, bufs, sems):
-        self.first, self.base, self.grads, self.out, self.bufs = first, base, grads, out, bufs
-        self.sems = sems
-        self.members = 2 * first.chips
-        self.chunk = size // self.members
-        me = 2 * first.chip + first.core
-        self.mine = first.rows(base + me * self.chunk, self.chunk)
-        self.others = [lax.rem(me + d, self.members) for d in range(self.members)]
-        self.peers = [
-            (m // 4, 4 * first.line + 2 * lax.rem(m // 2, 2) + lax.rem(m, 2)) for m in self.others
-        ]
-
-    def send(self, stage, items):
-        self.flying = []
-        for d, (src, dst, target) in enumerate(items):
-            copy = pltpu.make_async_remote_copy(
-                src_ref=src,
-                dst_ref=dst,
-                send_sem=self.sems.at[0, stage, d],
-                recv_sem=self.sems.at[1, stage, d],
-                device_id=target,
-                device_id_type=MESH,
-            )
-            copy.start()
-            self.flying.append(copy)
-
-    def wait(self):
-        for copy in self.flying:
-            copy.wait()
-
-    def plane(self):
-        items = []
-        for d in range(1, self.members):
-            away = self.first.rows(self.base + self.others[d] * self.chunk, self.chunk)
-            items.append((self.grads.at[away], self.bufs[0].at[d], self.peers[d]))
-        self.send(0, items)
-
-    def line(self):
-        self.wait()
-        slots, held = self.bufs
-        total = self.grads[self.mine, :].astype(F32)
-        for d in range(1, self.members):
-            total += slots[d].astype(F32)
-        here = self.first.rows(self.first.line * self.chunk, self.chunk)
-        held[here, :] = total.astype(BF16)
-        target = held.at[here]
-        self.send(1, [(target, target, peer) for peer in self.first.line_peers[1:]])
-
-    def back(self):
-        self.wait()
-        held = self.bufs[1]
-        total = held[0 : self.chunk, :].astype(F32)
-        for n in range(1, self.first.lines):
-            total += held[n * self.chunk : (n + 1) * self.chunk, :].astype(F32)
-        self.out[self.mine, :] = total.astype(BF16)
-        target = self.out.at[self.mine]
-        self.send(2, [(target, target, peer) for peer in self.peers[1:]])
+        target = self.out.at[self.rows(self.base + self.core * self.half, self.half)]
+        self.send(5, [(target, target, self.sibling)])
 
 
 def whole_kernel(
@@ -222,7 +161,7 @@
     order, t1, t2, o4, tg, w1, wb, wc, hgrads,
     *rest,
 ):
-    sems, quick_sems, local_sems, halo_sems = rest[8:]
+    sems, local_sems, halo_sems = rest[18:]
     me, sample = lax.axis_index("space"), lax.axis_index("sample")
     has_low, has_high = me > 0, me < spaces - 1
     below, above = me - 1, me + 1
@@ -236,8 +175,11 @@
         item.start()
 
     _, _, streams = plan(samples, spaces)
-    first = Sum(*streams[0], samples, spaces, grads, out, rest[0:6], sems)
-    second = QuickSum(first, *streams[1], grads, out, rest[6:8], quick_sems)
+    sums = [
+        Sum(stream, samples, spaces, grads, out, rest[6 * n : 6 * n + 6], sems.at[n])
+        for n, stream in enumerate(streams)
+    ]
+    first, second, late = sums
     barrier = pltpu.get_barrier_semaphore()
 
     @pl.when(has_low)
@@ -248,7 +190,7 @@
     def _():
         pl.semaphore_signal(barrier, inc=1, device_id=(sample, above), device_id_type=MESH)
 
-    peers = second.peers[1:] + first.line_peers[1:]
+    peers = first.peers()
     for peer in peers:
         pl.semaphore_signal(barrier, inc=1, device_id=peer, device_id_type=MESH)
     near = jnp.minimum(me, 1) + jnp.minimum(spaces - 1 - me, 1)
@@ -382,6 +324,7 @@
         here = t2[:, 256 * dz : 256 * dz + 256]
         grads[576 * dz : 576 * dz + 576, :] = mm(here, og[...], nt).astype(BF16)
     first.pair()
+    second.pair()
 
     total = jnp.zeros((128, 256), F32)
     for dz in range(3):
@@ -393,7 +336,8 @@
     pre_grads = jnp.where(real, slope, 0.0).astype(BF16)
     pre_wide = pre_grads.astype(F32)
 
-    first.plane()
+    first.first_level()
+    second.first_level()
 
     pairs = {}
     for dz in range(3):
@@ -414,12 +358,14 @@
     used = ROWS_TWO + ROWS_ONE
     if grads.shape[0] > used:
         grads[used:, :] = jnp.zeros((grads.shape[0] - used, 128), BF16)
-    second.plane()
+    late.pair()
 
     for index, part in enumerate(
         windows(lambda ph: pre_wide[64 * ph : 64 * ph + 64, :], 1024, us)
     ):
         tg[64 * index : 64 * index + 64, :] = part
+    late.first_level()
+
     back = mm(wc[0], tg[:, 512:1024]) + mm(wc[1], tg[:, 256:768]) + mm(wc[2], tg[:, 0:512])
     back = back.astype(BF16)
     for z in range(2):
@@ -428,14 +374,16 @@
         )
         igrads[z] = mm(plane_rows, order[...], nt).astype(BF16)
 
-    first.line_sum()
-    second.line()
-    first.line_back()
-    second.back()
-    first.plane_back()
-    first.pair_back()
-    second.wait()
-    first.wait()
+    for item in sums:
+        item.second_level()
+    for item in sums:
+        item.second_back()
+    for item in sums:
+        item.first_back()
+    for item in sums:
+        item.pair_back()
+    for item in sums:
+        item.wait()
 
 
 def tail_kernel(scale_one, scale_two, layer, igrads, summed, layer_out, igrads_out, first, second):
@@ -457,10 +405,19 @@
     vol = volume.reshape(depth, channels_in, plane)
     og = out_grads.reshape(128, 256)
     chips, lines, streams = plan(samples, spaces)
-    rows = streams[1][0] + streams[1][1]
-    early, late = streams[0][1], streams[1][1]
-    half, chunk = early // 2, early // 2 // chips
-    part, quick = line_rows(early, chips, lines), late // 2 // chips
+    rows = streams[2][0] + streams[2][1]
+    buffers = []
+    for _, size, line_first in streams:
+        outer, inner = (lines, chips) if line_first else (chips, lines)
+        chunk, piece = level_rows(size, outer, inner)
+        buffers += [
+            pltpu.VMEM((size // 2, 128), BF16),
+            pltpu.VMEM((size // 2, 128), BF16),
+            pltpu.VMEM((outer, chunk, 128), BF16),
+            pltpu.VMEM((inner * piece, 128), BF16),
+            pltpu.VMEM((inner, piece, 128), BF16),
+            pltpu.VMEM((inner * piece, 128), BF16),
+        ]
     layer, igrads, summed = pl.pallas_call(
         functools.partial(whole_kernel, samples, spaces),
         out_shape=[
@@ -489,16 +446,8 @@
             pltpu.VMEM((3, 256, 512), BF16),
             pltpu.VMEM((3, 128, 1024), BF16),
             pltpu.VMEM((256, 1024), BF16),
-            pltpu.VMEM((half, 128), BF16),
-            pltpu.VMEM((half, 128), BF16),
-            pltpu.VMEM((chips, chunk, 128), BF16),
-            pltpu.VMEM((lines * part, 128), BF16),
-            pltpu.VMEM((lines, part, 128), BF16),
-            pltpu.VMEM((lines * part, 128), BF16),
-            pltpu.VMEM((2 * chips, quick, 128), BF16),
-            pltpu.VMEM((lines * quick, 128), BF16),
-            pltpu.SemaphoreType.DMA((2, 6, max(chips, lines))),
-            pltpu.SemaphoreType.DMA((2, 3, max(2 * chips, lines))),
+            *buffers,
+            pltpu.SemaphoreType.DMA((3, 2, 6, max(chips, lines))),
             pltpu.SemaphoreType.DMA((4,)),
             pltpu.SemaphoreType.DMA((2, 4)),
         ],

time: 39.8 us -> 36.5 us (0.917)
  Pallas kernels: 39 us -> 35.7 us
    pallas_call x1, Pallas kernels: 36.6 us -> 33.4 us  [local(): pl.pallas_call(functools.partial(whole_kernel, samples, spaces), out_shap...]
where the time goes in v4:
time: 36.5 us; the launch traced here: 36.4 us
  Pallas kernels  35.7 us (98%)
  between operations  0.64 us (2%)
    pallas_call x1, Pallas kernels, local(): pl.pallas_call(functools.partial(whole_kernel, samples, spaces), out_shap...  33.4 us
    pallas_call x1, Pallas kernels, local(): pl.pallas_call(functools.partial(tail_kernel, scale_one, scale_two), out_...  2.37 us

profile of v4, /device:TPU:0, one launch (start us, length us, event | category | flops | bytes accessed | tf_op | source)
XLA Modules:
  0.0 36.4 jit_solution(5522677870011738465)
XLA Ops:
  0.6 33.4 %conv_pair.1 = (bf16[128,256]{1,0:T(8,128)(2,1)}, bf16[2,32,1024]{2,1,0:T(8,128)(2,1)}, bf16[2176,128]{1,0:T(8,128)(2,1)}) custom-call(bf16[2,32,1024]{2,1,0:T(8,128)(2,1)} %bitcast.7, bf16[128,256]{1,0:T(8,128)(2,1)} %bitcast.8, bf16[27,32,64]{2,1,0:T(8,128)(2,1)} %k1_far.1, bf16[27,64,128]{2,1,0:T(8,128)(2,1)} %k2_far.1), custom_call_target="tpu_custom_call" | custom-call | tf_op jit(solution)/shard_map/conv_pair/pallas_call | solution.py:421
  34.0 2.4 %finish.1 = (bf16[128,256]{1,0:T(8,128)(2,1)}, bf16[2,32,1024]{2,1,0:T(8,128)(2,1)}, f32[27,32,64]{2,1,0:T(8,128)}, f32[1728,128]{1,0:T(8,128)}) custom-call(bf16[128,256]{1,0:T(8,128)(2,1)} %get-tuple-element.11.layer, bf16[2,32,1024]{2,1,0:T(8,128)(2,1)} %get-tuple-element.12.igrads, bf16[2176,128]{1,0:T(8,128)(2,1)} %get-tuple-element.13.summed), custom_call_target="tpu_custom_call" | custom-call | tf_op jit(solution)/shard_map/finish/pallas_call | solution.py:459

commit v5 on v4

--- a/solution.py
+++ b/solution.py
@@ -206,8 +206,12 @@
             device_id_type=MESH,
         )
 
-    up = [(og_far, olo, 0), (vol_far, vlo, 1)]
-    down = [(og_far, ohi, 2), (vol_far, vhi, 3)]
+    up = [(vol_far, vlo, 0), (og_far, olo, 1)]
+    down = [
+        (vol_far.at[0], vhi.at[0], 2),
+        (og_far, ohi, 3),
+        (vol_far.at[1], vhi.at[1], 4),
+    ]
 
     @pl.when(has_high)
     def _():
@@ -254,25 +258,66 @@
                 axis=1,
             )
 
-    def arrive(n):
+    def arrive(ups, downs):
         @pl.when(has_high)
         def _():
-            src, dst, index = up[n]
-            halo(src, dst, index, above).wait_send()
-            src, dst, index = down[n]
-            halo(src, dst, index, above).wait_recv()
+            for src, dst, index in ups:
+                halo(src, dst, index, above).wait_send()
+            for src, dst, index in downs:
+                halo(src, dst, index, above).wait_recv()
 
         @pl.when(has_low)
         def _():
-            src, dst, index = down[n]
-            halo(src, dst, index, below).wait_send()
-            src, dst, index = up[n]
-            halo(src, dst, index, below).wait_recv()
+            for src, dst, index in downs:
+                halo(src, dst, index, below).wait_send()
+            for src, dst, index in ups:
+                halo(src, dst, index, below).wait_recv()
 
     fetched[2].wait()
     fetched[3].wait()
-    arrive(0)
+    arrive(up[:1], down[:1])
     zero = jnp.zeros((), BF16)
+    low = jnp.where(has_low, vlo[...].reshape(64, 1024), zero)
+    high = jnp.where(has_high, vhi[0], zero)
+    cells = jnp.concatenate([low, vol[...].reshape(64, 1024), high], axis=0)
+    split = mm(cells, order[...])
+
+    def volume_part(phase):
+        return jnp.concatenate(
+            [split[32 * p : 32 * p + 32, 256 * phase : 256 * phase + 256] for p in range(5)], axis=1
+        )
+
+    for index, part in enumerate(windows(volume_part, 1280, us)):
+        t1[32 * index : 32 * index + 32, 0:1280] = part
+
+    tn = ((0,), (0,))
+    nt = ((1,), (1,))
+    pre = mm(w1[0], t1[:, 0:768], tn)
+    pre += mm(w1[1], t1[:, 256:1024], tn)
+    pre += mm(w1[2], t1[:, 512:1280], tn)
+    sigma = 1.0 / (1.0 + jnp.exp(-pre))
+    plane = lax.broadcasted_iota(jnp.int32, (1, 768), 1) >> 8
+    hidden = jnp.where((plane > 0) | has_low, pre * sigma, 0.0).astype(BF16).astype(F32)
+    for index, part in enumerate(
+        windows(lambda ph: hidden[64 * ph : 64 * ph + 64, 0:768], 768, (-1, 0, 1))
+    ):
+        t2[64 * index : 64 * index + 64, :] = part
+    for dz in range(3):
+        here = t2[:, 256 * dz : 256 * dz + 256]
+        grads[576 * dz : 576 * dz + 576, :] = mm(here, og[...], nt).astype(BF16)
+    first.pair()
+    second.pair()
+
+    total = jnp.zeros((128, 256), F32)
+    for dz in range(3):
+        here = t2[:, 256 * dz : 256 * dz + 256]
+        total += mm(k2[9 * dz : 9 * dz + 9].reshape(576, 128), here, tn)
+    layer[...] = total.astype(BF16)
+
+    first.first_level()
+    second.first_level()
+
+    arrive(up[1:], down[1:2])
     og_three = jnp.concatenate(
         [jnp.where(has_low, olo[...], zero), og[...], jnp.where(has_high, ohi[...], zero)], axis=1
     ).astype(F32)
@@ -293,51 +338,9 @@
     hgrads[:, 256:512] = even[:, 0:256].astype(BF16)
     hgrads[:, 512:768] = odd[:, 256:512].astype(BF16)
     hgrads[:, 768:1024] = even[:, 256:512].astype(BF16)
-    arrive(1)
-    low = jnp.where(has_low, vlo[...].reshape(64, 1024), zero)
-    high = jnp.where(has_high, vhi[...].reshape(64, 1024), zero)
-    cells = jnp.concatenate([low, vol[...].reshape(64, 1024), high], axis=0)
-    split = mm(cells, order[...])
-
-    def volume_part(phase):
-        return jnp.concatenate(
-            [split[32 * p : 32 * p + 32, 256 * phase : 256 * phase + 256] for p in range(6)], axis=1
-        )
-
-    for index, part in enumerate(windows(volume_part, 1536, us)):
-        t1[32 * index : 32 * index + 32, :] = part
-
-    tn = ((0,), (0,))
-    nt = ((1,), (1,))
-    pre = mm(w1[0], t1[:, 0:1024], tn)
-    pre += mm(w1[1], t1[:, 256:1280], tn)
-    pre += mm(w1[2], t1[:, 512:1536], tn)
-    sigma = 1.0 / (1.0 + jnp.exp(-pre))
-    plane = lax.broadcasted_iota(jnp.int32, (1, 1024), 1) >> 8
-    real = ((plane > 0) | has_low) & ((plane < 3) | has_high)
-    hidden = jnp.where(real, pre * sigma, 0.0).astype(BF16).astype(F32)
-    for index, part in enumerate(
-        windows(lambda ph: hidden[64 * ph : 64 * ph + 64, 0:768], 768, (-1, 0, 1))
-    ):
-        t2[64 * index : 64 * index + 64, :] = part
-    for dz in range(3):
-        here = t2[:, 256 * dz : 256 * dz + 256]
-        grads[576 * dz : 576 * dz + 576, :] = mm(here, og[...], nt).astype(BF16)
-    first.pair()
-    second.pair()
-
-    total = jnp.zeros((128, 256), F32)
-    for dz in range(3):
-        here = t2[:, 256 * dz : 256 * dz + 256]
-        total += mm(k2[9 * dz : 9 * dz + 9].reshape(576, 128), here, tn)
-    layer[...] = total.astype(BF16)
-
-    slope = hgrads[...].astype(F32) * sigma * (1.0 + pre * (1.0 - sigma))
-    pre_grads = jnp.where(real, slope, 0.0).astype(BF16)
-    pre_wide = pre_grads.astype(F32)
-
-    first.first_level()
-    second.first_level()
+
+    slope = hgrads[:, 0:768].astype(F32) * sigma * (1.0 + pre * (1.0 - sigma))
+    pre_grads = jnp.where((plane > 0) | has_low, slope, 0.0).astype(BF16)
 
     pairs = {}
     for dz in range(3):
@@ -360,6 +363,19 @@
         grads[used:, :] = jnp.zeros((grads.shape[0] - used, 128), BF16)
     late.pair()
 
+    arrive([], down[2:])
+    last = mm(jnp.where(has_high, vhi[1], zero), order[...])
+    for index, part in enumerate(
+        windows(lambda ph: last[:, 256 * ph : 256 * ph + 256], 256, us)
+    ):
+        t1[32 * index : 32 * index + 32, 1280:1536] = part
+    pre_last = mm(w1[0], t1[:, 768:1024], tn)
+    pre_last += mm(w1[1], t1[:, 1024:1280], tn)
+    pre_last += mm(w1[2], t1[:, 1280:1536], tn)
+    sigma_last = 1.0 / (1.0 + jnp.exp(-pre_last))
+    slope = hgrads[:, 768:1024].astype(F32) * sigma_last * (1.0 + pre_last * (1.0 - sigma_last))
+    slope = jnp.where(has_high, slope, 0.0).astype(BF16)
+    pre_wide = jnp.concatenate([pre_grads, slope], axis=1).astype(F32)
     for index, part in enumerate(
         windows(lambda ph: pre_wide[64 * ph : 64 * ph + 64, :], 1024, us)
     ):
@@ -449,7 +465,7 @@
             *buffers,
             pltpu.SemaphoreType.DMA((3, 2, 6, max(chips, lines))),
             pltpu.SemaphoreType.DMA((4,)),
-            pltpu.SemaphoreType.DMA((2, 4)),
+            pltpu.SemaphoreType.DMA((2, 5)),
         ],
         compiler_params=pltpu.CompilerParams(
             collective_id=0, has_side_effects=True, vmem_limit_bytes=56 * 2**20

time: 36.5 us -> 36.7 us (level)
  no operation moved by 1% of the time
where the time goes in v5:
time: 36.7 us; the launch traced here: 36.6 us
  Pallas kernels  35.9 us (98%)
  between operations  0.64 us (2%)
    pallas_call x1, Pallas kernels, local(): pl.pallas_call(functools.partial(whole_kernel, samples, spaces), out_shap...  33.5 us
    pallas_call x1, Pallas kernels, local(): pl.pallas_call(functools.partial(tail_kernel, scale_one, scale_two), out_...  2.37 us

profile of v5, /device:TPU:0, one launch (start us, length us, event | category | flops | bytes accessed | tf_op | source)
XLA Modules:
  0.0 36.6 jit_solution(7592633375010319898)
XLA Ops:
  0.6 33.5 %conv_pair.1 = (bf16[128,256]{1,0:T(8,128)(2,1)}, bf16[2,32,1024]{2,1,0:T(8,128)(2,1)}, bf16[2176,128]{1,0:T(8,128)(2,1)}) custom-call(bf16[2,32,1024]{2,1,0:T(8,128)(2,1)} %bitcast.7, bf16[128,256]{1,0:T(8,128)(2,1)} %bitcast.8, bf16[27,32,64]{2,1,0:T(8,128)(2,1)} %k1_far.1, bf16[27,64,128]{2,1,0:T(8,128)(2,1)} %k2_far.1), custom_call_target="tpu_custom_call" | custom-call | tf_op jit(solution)/shard_map/conv_pair/pallas_call | solution.py:437
  34.2 2.4 %finish.1 = (bf16[128,256]{1,0:T(8,128)(2,1)}, bf16[2,32,1024]{2,1,0:T(8,128)(2,1)}, f32[27,32,64]{2,1,0:T(8,128)}, f32[1728,128]{1,0:T(8,128)}) custom-call(bf16[128,256]{1,0:T(8,128)(2,1)} %get-tuple-element.11.layer, bf16[2,32,1024]{2,1,0:T(8,128)(2,1)} %get-tuple-element.12.igrads, bf16[2176,128]{1,0:T(8,128)(2,1)} %get-tuple-element.13.summed), custom_call_target="tpu_custom_call" | custom-call | tf_op jit(solution)/shard_map/finish/pallas_call | solution.py:475
